TPU v7x, 32 devices: a whole 2x2x4 slice. The times are simulated.
32 devices in a mesh: seq: 8 (over z, y), tp: 4 (over x, core).
Axes of the slice: x: 2, y: 2, z: 4, core: 2. Of those that a mesh axis runs over, the one named last changes fastest.
Arguments:
- tokens: bfloat16 [4096, 768], P('seq'), may hold values from -6 to 6
- cotangent: bfloat16 [4096, 768], P('seq'), may hold values from -6 to 6
- past_states: bfloat16 [4096, 768], P('seq'), may hold values from -6 to 6
- doc_ids: int32 [4096], P('seq'), may hold values from 0 to 4095, as said below
- cur_book: int32 [8], P('seq'), may hold values from 0 to 3
- past_book: int32 [8], P('seq'), may hold values from 0 to 3, as said below
- past_age: int32 [8], P('seq'), may hold values from 0 to 1, as said below
- ln1_gain: float32 [768], replicated, may hold values from 0.5 to 1.5
- ln1_bias: float32 [768], replicated, may hold values from -3 to 3
- qkv_weight: bfloat16 [768, 3, 768], P(None, None, 'tp'), may hold values from -0.21875 to 0.21875
- qv_bias: float32 [2, 768], P(None, 'tp'), may hold values from -3 to 3
- out_weight: bfloat16 [768, 768], P('tp'), may hold values from -0.75 to 0.75
- out_bias: float32 [768], replicated, may hold values from -3 to 3
- ln2_gain: float32 [768], replicated, may hold values from 0.5 to 1.5
- ln2_bias: float32 [768], replicated, may hold values from -3 to 3
- fc_weight: bfloat16 [768, 3072], P(None, 'tp'), may hold values from -0.21875 to 0.21875
- fc_bias: float32 [3072], P('tp'), may hold values from -3 to 3
- proj_weight: bfloat16 [3072, 768], P('tp'), may hold values from -0.109375 to 0.109375
- proj_bias: float32 [768], replicated, may hold values from -3 to 3
- mu_weight: float32 [12, 512], P('tp'), may hold values from -0.25 to 0.25
- sigma_weight: float32 [12, 512], P('tp'), may hold values from -0.25 to 0.25
Outputs:
- output: bfloat16 [4096, 768], P('seq')
- grad_tokens: bfloat16 [4096, 768], P('seq')
- grad_qkv_weight: float32 [768, 3, 768], P('seq', None, 'tp')
- grad_qv_bias: float32 [2, 768], P(None, 'tp')
- grad_out_weight: float32 [768, 768], P('tp', 'seq')
- grad_out_bias: float32 [768], replicated
- grad_fc_weight: float32 [768, 3072], P('seq', 'tp')
- grad_fc_bias: float32 [3072], P('tp')
- grad_proj_weight: float32 [3072, 768], P('tp', 'seq')
- grad_proj_bias: float32 [768], replicated
- grad_ln1_gain: float32 [768], replicated
- grad_ln1_bias: float32 [768], replicated
- grad_ln2_gain: float32 [768], replicated
- grad_ln2_bias: float32 [768], replicated
- grad_mu_weight: float32 [12, 512], P('tp')
- grad_sigma_weight: float32 [12, 512], P('tp')
Inputs may be any that keep to these rules, and one draw needn't show every extreme that they name: `doc_ids`: each token's value is the position of the last token of its document, so values never fall along the tokens. One document starts inside the first 512 tokens and ends inside the last 512; the others are short. `past_book`: each of the 4 books has exactly 2 past segments. `past_age`: within each book the ages of its past segments are 0 to 1, each once.
All inputs are finite; a program needn't handle non-finite values.
Results may differ from a plain program's by a relative error of at most 0.019.
Values may be sent and summed in bfloat16 or wider, within the bound.
A program may use at most 128 MiB of HBM per device.

v0:
```python
import functools
from typing import NamedTuple

import ml_dtypes
import numpy as np

import jax
import jax.numpy as jnp
from jax import lax
from jax.experimental import pallas as pl
from jax.experimental.pallas import tpu as pltpu
from jax.sharding import PartitionSpec as P

D = 768
DH = 64
NB = 512
SEG = 512
BOOKS = 4


EPS = 1e-05
TAU = 0.75
RIDGE = 1.0
SPREAD = 0.01
NEGATIVE = -1e30
MESH_ID = pl.DeviceIdType.MESH
VMEM_LIMIT = 60 * 2**20


def coefficient_tables(age_count, basis_n, seg_len):
    shrink = TAU ** np.arange(age_count, dtype=np.float64)
    inside = (np.arange(seg_len) + 0.5) / seg_len
    times = shrink[:, None] * (TAU + (1.0 - TAU) * inside[None, :])
    centres = (np.arange(basis_n) + 0.5) / basis_n
    offset = (times[:, None, :] - centres[None, :, None]) * basis_n
    basis = np.exp(-0.5 * offset * offset)
    gram = np.einsum("agx,ahx->gh", basis, basis) + RIDGE * np.eye(basis_n)
    table = np.linalg.solve(gram[None], basis)
    high = table.astype(ml_dtypes.bfloat16)
    lower = (table - high.astype(np.float64)).astype(ml_dtypes.bfloat16)
    return high, lower


LANES_OUT = 256


def head_of_lane(width):
    return lax.broadcasted_iota(jnp.int32, (1, width), 1) // DH


def head_masks(width):
    lane_head = head_of_lane(width)
    return [(lane_head == head).astype(jnp.float32).astype(jnp.bfloat16) for head in range(width // DH)]


def pick_heads(per_head, lane_head):
    chosen = per_head[0]
    for head in range(1, len(per_head)):
        chosen = jnp.where(lane_head == head, per_head[head], chosen)
    return chosen


def dot_rows(left, right):
    return lax.dot_general(left, right, (((1,), (1,)), ((), ())), preferred_element_type=jnp.float32)


def dot_plain(left, right):
    return lax.dot_general(left, right, (((1,), (0,)), ((), ())), preferred_element_type=jnp.float32)


def thirds(value):
    first = value.astype(jnp.bfloat16)
    rest = value - first.astype(jnp.float32)
    second = rest.astype(jnp.bfloat16)
    third = (rest - second.astype(jnp.float32)).astype(jnp.bfloat16)
    return first, second, third


def with_stats(block, stats):
    rows, width = block.shape
    spare = LANES_OUT - width
    lane = lax.broadcasted_iota(jnp.int32, (1, spare), 1)
    tail = jnp.zeros((rows, spare), jnp.float32)
    for index, column in enumerate(stats):
        for part, value in enumerate(thirds(column)):
            tail = jnp.where(lane == 3 * index + part, value.astype(jnp.float32), tail)
    return jnp.concatenate([block, tail.astype(jnp.bfloat16)], axis=1)


def stat_column(extended, width, index):
    lane = lax.broadcasted_iota(jnp.int32, (1, LANES_OUT), 1)
    start = width + 3 * index
    mine = (lane >= start) & (lane < start + 3)
    return jnp.sum(jnp.where(mine, extended.astype(jnp.float32), 0.0), axis=1, keepdims=True)


def stat_rows(extended, width, count):
    row = lax.broadcasted_iota(jnp.int32, (count, LANES_OUT), 0)
    lane = lax.broadcasted_iota(jnp.int32, (count, LANES_OUT), 1)
    start = width + 3 * row
    chooser = ((lane >= start) & (lane < start + 3)).astype(jnp.float32).astype(jnp.bfloat16)
    return dot_rows(chooser, extended)


def greet(levels, whole_tp=False):
    seq, tp = lax.axis_index("seq"), lax.axis_index("tp")
    level, side = seq // 2, seq % 2
    barrier = pltpu.get_barrier_semaphore()
    pl.semaphore_signal(barrier, inc=1, device_id=(2 * level + 1 - side, tp), device_id_type=MESH_ID)

    def one(step, unused):
        other = lax.rem(level + step, levels)
        pl.semaphore_signal(barrier, inc=1, device_id=(2 * other + side, tp), device_id_type=MESH_ID)
        return unused

    lax.fori_loop(1, levels, one, 0)
    if not whole_tp:
        return barrier, levels
    greet_tp()
    return barrier, levels + 2


class MemoryPlace(NamedTuple):
    loose: jax.Array
    centre: jax.Array
    spread: jax.Array
    height: jax.Array
    gap: jax.Array


def memory_place(query, spot_rows, in_head):
    width_sq = 1.0 / (NB * NB)
    centre = 1.0 / (
        1.0 + jnp.exp(-jnp.sum(jnp.where(in_head, query * spot_rows[0:1, :], 0.0), axis=1, keepdims=True))
    )
    loose = jnp.sum(jnp.where(in_head, query * spot_rows[1:2, :], 0.0), axis=1, keepdims=True)
    soft = jnp.maximum(loose, 0.0) + jnp.log(1.0 + jnp.exp(-jnp.abs(loose)))
    spread = SPREAD * soft + width_sq
    height = (1.0 / NB) * lax.rsqrt(spread)
    centres = (lax.broadcasted_iota(jnp.int32, (1, NB), 1).astype(jnp.float32) + 0.5) / NB
    return MemoryPlace(loose, centre, spread, height, centre - centres)


def forward_kernel(
    levels,
    tok_ref,
    norm_ref,
    weight_ref,
    bias_ref,
    doc_col_ref,
    doc_row_ref,
    key_mask_ref,
    past_ref,
    book_ref,
    spot_ref,
    table_ref,
    normed_ref,
    query_out_ref,
    kv_out_ref,
    out_ref,
    lse_ref,
    heads_ref,
    coeff_ref,
    mem_ref,
    spot_row_ref,
    pair_ref,
    top_ref,
    total_ref,
    acc_ref,
    part_ref,
    part_in_ref,
    kv_send,
    kv_recv,
    q_send,
    q_recv,
    pair_sem,
    part_sem,
    past_col_ref,
    past_oth_ref,
    table_in_ref,
    past_up,
    past_down,
    past_side,
    coeff_sems,
    table_sem,
):
    seq, tp = lax.axis_index("seq"), lax.axis_index("tp")
    level, side = seq // 2, seq % 2
    rows = tok_ref.shape[0]
    width = pair_ref.shape[2]
    heads = width // DH
    partner = (2 * level + 1 - side, tp)
    lane_head = head_of_lane(width)
    head_mask = head_masks(width)
    barrier, greetings = greet(levels, True)

    chunk = rows // 2
    past_col_ref[level] = past_ref[...]

    def past_copy(direction, from_level):
        block = past_col_ref.at[from_level]
        if direction == "side":
            sems, target, place = past_side, partner, past_oth_ref.at[from_level]
        elif direction == "up":
            sems, target, place = past_up, (lax.rem(2 * level + 2, 2 * levels) + side, tp), block
        else:
            sems, target, place = past_down, (lax.rem(2 * (level + levels - 1), 2 * levels) + side, tp), block
        return pltpu.make_async_remote_copy(
            block,
            place,
            sems.at[0, from_level],
            sems.at[1, from_level],
            device_id=target,
            device_id_type=MESH_ID,
        )

    pl.semaphore_wait(barrier, greetings)

    def pass_past(from_level, up, down):
        past_copy("side", from_level).start()
        if up:

            @pl.when(level < levels - 1)
            def _():
                past_copy("up", from_level).start()

        if down:

            @pl.when(level > 0)
            def _():
                past_copy("down", from_level).start()

    pass_past(level, True, True)

    def project(index, unused):
        here = pl.ds(pl.multiple_of(index * chunk, chunk), chunk)
        x = tok_ref[here, :].astype(jnp.float32)
        centred = x - jnp.mean(x, axis=1, keepdims=True)
        variance = jnp.mean(centred * centred, axis=1, keepdims=True)
        a = centred * lax.rsqrt(variance + EPS) * norm_ref[0:1, :] + norm_ref[1:2, :]
        a = a.astype(jnp.bfloat16)
        normed_ref[here, :] = a
        mixed = (dot_plain(a, weight_ref[...]) + bias_ref[0:1, :]).astype(jnp.bfloat16)
        query = mixed[:, :width] * jnp.bfloat16(DH**-0.5)
        pair_ref[0, here, :] = query
        query_out_ref[level, here, :] = query
        kv_out_ref[level, here, :] = mixed[:, width:]
        return unused

    lax.fori_loop(0, rows // chunk, project, 0)
    kv_out_ref[level, rows:, :] = key_mask_ref[...]

    pair_copy = pltpu.make_async_remote_copy(
        pair_ref.at[0], pair_ref.at[1], pair_sem.at[0], pair_sem.at[1], device_id=partner, device_id_type=MESH_ID
    )
    pair_copy.start()

    def kv_copy(from_level):
        return pltpu.make_async_remote_copy(
            kv_out_ref.at[from_level],
            kv_out_ref.at[from_level],
            kv_send.at[from_level],
            kv_recv.at[from_level],
            device_id=(lax.rem(2 * level + 2, 2 * levels) + side, tp),
            device_id_type=MESH_ID,
        )

    def query_copy(from_level, to_level):
        return pltpu.make_async_remote_copy(
            query_out_ref.at[from_level],
            query_out_ref.at[from_level],
            q_send.at[to_level],
            q_recv.at[from_level],
            device_id=(2 * to_level + side, tp),
            device_id_type=MESH_ID,
        )

    @pl.when(level < levels - 1)
    def _():
        kv_copy(level).start()

    def send_down(step, unused):
        query_copy(level, level - step).start()
        return unused

    lax.fori_loop(1, level + 1, send_down, 0)

    top_ref[...] = jnp.full(top_ref.shape, NEGATIVE, jnp.float32)
    total_ref[...] = jnp.zeros(total_ref.shape, jnp.float32)
    acc_ref[...] = jnp.zeros(acc_ref.shape, jnp.float32)

    doc_first = doc_row_ref[0:1, 0:1]
    def reach_of(here):
        docs = doc_col_ref[here, :]
        last = (level == levels - 1) & (side == 1)
        return jnp.where(last & (docs != doc_first), NEGATIVE, 0.0)

    def fold(slot, from_level, mask_kind):
        mask_rows = kv_out_ref[from_level, rows:, :].astype(jnp.float32)
        key_mask = jnp.concatenate([mask_rows[0:1, : rows // 2], mask_rows[1:2, : rows // 2]], axis=1)

        def part(index, unused):
            here = pl.ds(pl.multiple_of(index * chunk, chunk), chunk)
            query = pair_ref[slot, here, :]
            keys = kv_out_ref[from_level, :rows, :width]
            vals = kv_out_ref[from_level, :rows, width:]
            if mask_kind == "own":
                q_pos = index * chunk + lax.broadcasted_iota(jnp.int32, (chunk, rows), 0)
                k_pos = lax.broadcasted_iota(jnp.int32, (chunk, rows), 1)
                visible = (q_pos >= k_pos) & (doc_col_ref[here, :] == doc_row_ref[0:1, :])
            products, scales = [], []
            for head in range(heads):
                scores = dot_rows(query * head_mask[head], keys)
                old_top = top_ref[slot, head, here, :]
                if mask_kind == "own":
                    scores = jnp.where(visible, scores, NEGATIVE)
                    reach = 0.0
                else:
                    scores = scores + key_mask
                    reach = jnp.where(slot == 0, reach_of(here), 0.0)
                new_top = jnp.maximum(old_top, jnp.max(scores, axis=1, keepdims=True) + reach)
                weights = jnp.exp(scores - (new_top - reach))
                scale = jnp.exp(old_top - new_top)
                top_ref[slot, head, here, :] = new_top
                total_ref[slot, head, here, :] = total_ref[slot, head, here, :] * scale + jnp.sum(
                    weights, axis=1, keepdims=True
                )
                products.append(dot_plain(weights.astype(jnp.bfloat16), vals))
                scales.append(scale)
            acc_ref[slot, here, :] = acc_ref[slot, here, :] * pick_heads(scales, lane_head) + pick_heads(
                products, lane_head
            )
            return unused

        lax.fori_loop(0, rows // chunk, part, 0)

    fold(0, level, "own")
    pair_copy.wait()

    @pl.when(side == 0)
    def _():
        fold(1, level, "off")

    def keys_arrived(step):
        from_level = level - step
        kv_copy(from_level).wait_recv()

        @pl.when(level < levels - 1)
        def _():
            kv_copy(from_level).start()

        def both(slot, inner):
            fold(slot, from_level, "off")
            return inner

        lax.fori_loop(0, 2, both, 0)

    def arrived(step, unused):
        @pl.when(level >= step)
        def _():
            past_copy("up", level - step).wait_recv()
            pass_past(level - step, True, False)

        @pl.when(level + step < levels)
        def _():
            past_copy("down", level + step).wait_recv()
            pass_past(level + step, False, True)

        @pl.when((level >= step) & (step < levels - 1))
        def _():
            keys_arrived(step)

        return unused

    lax.fori_loop(1, levels, arrived, 0)

    def from_side(other, unused):
        past_copy("side", other).wait_recv()
        return unused

    lax.fori_loop(0, levels, from_side, 0)
    own_book = book_ref[0:1, :]
    time_half = rows // 2
    ages = table_ref.shape[0]

    def one_age(age, total):
        table_copy = pltpu.make_async_copy(table_ref.at[age], table_in_ref, table_sem)
        table_copy.start()

        def one_level(other, found):
            for blocks_ref in (past_col_ref, past_oth_ref):
                mark = blocks_ref[other, time_half:, :].astype(jnp.float32)
                chosen = (mark[0:1, :] == own_book) & (mark[1:2, :] == age.astype(jnp.float32))
                found = jnp.where(chosen, blocks_ref[other, :time_half, :].astype(jnp.float32), found)
            return found

        found = lax.fori_loop(
            0, levels, one_level, jnp.zeros((time_half, 2 * width), jnp.float32)
        ).astype(jnp.bfloat16)
        table_copy.wait()
        for index in range(2):
            table = table_in_ref[index]
            total = total + (
                dot_plain(table[:, :time_half], found)[:, :width]
                + dot_plain(table[:, time_half:], found)[:, width:]
            )
        return total

    coeff = lax.fori_loop(0, ages, one_age, jnp.zeros((NB, width), jnp.float32))
    coeff_ref[tp] = coeff.astype(jnp.bfloat16)

    def coeff_copy(kind, slot, index):
        return swap_with(kind, coeff_ref.at[slot], coeff_ref.at[slot], (coeff_sems.at[0], coeff_sems.at[1]), index)

    core_mate, chip_mate = tp + 1 - 2 * (tp % 2), lax.rem(tp + 2, 4)
    coeff_copy("chip", tp, 0).start()
    coeff_copy("core", tp, 1).start()

    @pl.when(level == levels - 1)
    def _():
        keys_arrived(levels - 1)

    def finish(index, unused):
        here = pl.ds(pl.multiple_of(index * chunk, chunk), chunk)
        totals = [total_ref[1, head, here, :] for head in range(heads)]
        tops = [top_ref[1, head, here, :] for head in range(heads)]
        some = [value > 0.0 for value in totals]
        inverse = [jnp.where(ok, 1.0 / jnp.where(ok, value, 1.0), 0.0) for ok, value in zip(some, totals)]
        logs = [
            jnp.where(ok, top + jnp.log(jnp.where(ok, value, 1.0)), NEGATIVE)
            for ok, top, value in zip(some, tops, totals)
        ]
        share = (acc_ref[1, here, :] * pick_heads(inverse, lane_head)).astype(jnp.bfloat16)
        part_ref[here, :] = with_stats(share, logs)
        return unused

    lax.fori_loop(0, rows // chunk, finish, 0)
    part_copy = pltpu.make_async_remote_copy(
        part_ref, part_in_ref, part_sem.at[0], part_sem.at[1], device_id=partner, device_id_type=MESH_ID
    )
    part_copy.start()

    coeff_copy("chip", chip_mate, 0).wait_recv()
    coeff_copy("core", chip_mate, 2).start()
    coeff_copy("core", core_mate, 1).wait_recv()
    coeff_copy("core", lax.rem(core_mate + 2, 4), 2).wait_recv()
    memory = jnp.zeros((NB, 2 * width), jnp.float32)
    for slot in range(4):
        memory = memory + dot_plain(
            coeff_ref[slot], weight_ref[slot * width : (slot + 1) * width, width:]
        )
    mem_ref[...] = memory.astype(jnp.bfloat16)
    for index in range(2):
        spots = spot_ref[8 * index : 8 * index + 8, :]
        row = sum(dot_plain(third, mem_ref[:, :width]) for third in thirds(spots))
        spot_row_ref[index : index + 1, :] = pick_heads(
            [row[head : head + 1, :] for head in range(heads)], lane_head
        )
    part_copy.wait()

    def merge(index, unused):
        here = pl.ds(pl.multiple_of(index * chunk, chunk), chunk)
        reach = reach_of(here)
        received = part_in_ref[here, :]
        mine, theirs, columns = [], [], []
        for head in range(heads):
            total = total_ref[0, head, here, :]
            own_log = top_ref[0, head, here, :] + jnp.log(total)
            other_log = stat_column(received, width, head) + reach
            high = jnp.maximum(own_log, other_log)
            both_log = high + jnp.log(jnp.exp(own_log - high) + jnp.exp(other_log - high))
            mine.append(jnp.exp(own_log - both_log) / total)
            theirs.append(jnp.exp(other_log - both_log))
            columns.append(both_log)
        attended = acc_ref[0, here, :] * pick_heads(mine, lane_head) + received[:, :width].astype(
            jnp.float32
        ) * pick_heads(theirs, lane_head)
        out_ref[here, :] = attended
        query = pair_ref[0, here, :].astype(jnp.float32)
        reads = []
        for head in range(heads):
            place = memory_place(query, spot_row_ref[0:2, :], lane_head == head)
            density = place.height * jnp.exp(place.gap * place.gap * (-0.5 / place.spread))
            reads.append(dot_plain(density.astype(jnp.bfloat16), mem_ref[:, width:]))
        heads_ref[here, :] = (attended + pick_heads(reads, lane_head)).astype(jnp.bfloat16)
        lane = lax.broadcasted_iota(jnp.int32, (1, 8), 1)
        packed = jnp.zeros((chunk, 8), jnp.float32)
        for head in range(heads):
            packed = jnp.where(lane == head, columns[head], packed)
        lse_ref[here, :] = packed
        return unused

    lax.fori_loop(0, rows // chunk, merge, 0)

    coeff_copy("chip", tp, 0).wait_send()
    coeff_copy("core", tp, 1).wait_send()
    coeff_copy("core", chip_mate, 2).wait_send()

    def past_sent(other, unused):
        past_copy("side", other).wait_send()

        @pl.when((level < levels - 1) & (other <= level))
        def _():
            past_copy("up", other).wait_send()

        @pl.when((level > 0) & (other >= level))
        def _():
            past_copy("down", other).wait_send()

        return unused

    lax.fori_loop(0, levels, past_sent, 0)

    def sent_down(step, unused):
        query_copy(level, level - step).wait_send()
        return unused

    lax.fori_loop(1, level + 1, sent_down, 0)

    def from_above(step, unused):
        query_copy(level + step, level).wait_recv()
        return unused

    lax.fori_loop(1, levels - level, from_above, 0)

    @pl.when(level < levels - 1)
    def _():
        def sent_up(from_level, unused):
            kv_copy(from_level).wait_send()
            return unused

        lax.fori_loop(0, level + 1, sent_up, 0)


def attention_forward(levels, tokens, norm, weight, bias, doc_ids, key_mask, past, book, spots, table):
    rows = tokens.shape[0]
    width = weight.shape[1] // 3
    heads = width // DH
    vmem = pl.BlockSpec(memory_space=pltpu.VMEM)
    dma = pltpu.SemaphoreType.DMA
    return pl.pallas_call(
        functools.partial(forward_kernel, levels),
        out_shape=(
            jax.ShapeDtypeStruct((rows, D), jnp.bfloat16),
            jax.ShapeDtypeStruct((levels, rows, width), jnp.bfloat16),
            jax.ShapeDtypeStruct((levels, rows + 16, 2 * width), jnp.bfloat16),
            jax.ShapeDtypeStruct((rows, width), jnp.float32),
            jax.ShapeDtypeStruct((rows, 8), jnp.float32),
            jax.ShapeDtypeStruct((rows, width), jnp.bfloat16),
            jax.ShapeDtypeStruct((4, NB, width), jnp.bfloat16),
            jax.ShapeDtypeStruct((NB, 2 * width), jnp.bfloat16),
            jax.ShapeDtypeStruct((8, width), jnp.float32),
        ),
        in_specs=[vmem] * 10 + [pl.BlockSpec(memory_space=pl.ANY)],
        out_specs=(vmem,) * 9,
        scratch_shapes=[
            pltpu.VMEM((2, rows, width), jnp.bfloat16),
            pltpu.VMEM((2, heads, rows, 1), jnp.float32),
            pltpu.VMEM((2, heads, rows, 1), jnp.float32),
            pltpu.VMEM((2, rows, width), jnp.float32),
            pltpu.VMEM((rows, LANES_OUT), jnp.bfloat16),
            pltpu.VMEM((rows, LANES_OUT), jnp.bfloat16),
            dma((levels,)),
            dma((levels,)),
            dma((levels,)),
            dma((levels,)),
            dma((2,)),
            dma((2,)),
            pltpu.VMEM((levels,) + past.shape, jnp.bfloat16),
            pltpu.VMEM((levels,) + past.shape, jnp.bfloat16),
            pltpu.VMEM(table.shape[1:], jnp.bfloat16),
            dma((2, levels)),
            dma((2, levels)),
            dma((2, levels)),
            dma((2, 3)),
            dma(()),
        ],
        name="attention_forward",
        compiler_params=pltpu.CompilerParams(
            collective_id=1, has_side_effects=True, vmem_limit_bytes=VMEM_LIMIT
        ),
    )(
        tokens,
        norm,
        weight,
        bias,
        doc_ids[:, None],
        doc_ids[None, :],
        key_mask,
        past,
        book,
        spots,
        table,
    )


def backward_kernel(
    levels,
    grad_ref,
    attended_ref,
    lse_ref,
    query_col_ref,
    query_oth_ref,
    kv_col_ref,
    kv_oth_ref,
    doc_col_ref,
    doc_row_ref,
    proj_blocks_ref,
    fc_blocks_ref,
    out_blocks_ref,
    base_ref,
    own_two_ref,
    other_two_ref,
    normed_ref,
    coeff_ref,
    mem_ref,
    spot_row_ref,
    spot_ref,
    grads_ref,
    weight_grad_ref,
    bias_grad_ref,
    spot_grad_ref,
    proj_share_ref,
    fc_share_ref,
    out_share_ref,
    output_ref,
    dq_ref,
    dk_ref,
    dv_ref,
    mem_acc_ref,
    pull_ref,
    own_ref,
    grad_col_ref,
    grad_oth_ref,
    stat_ref,
    col_send,
    col_recv,
    oth_send,
    oth_recv,
    *rest,
):
    scatters = []
    for blocks_ref in (proj_blocks_ref, fc_blocks_ref, out_blocks_ref):
        scatters.append(Scatter(levels, blocks_ref, *rest[:3], rest[3:7]))
        rest = rest[7:]
    late = LateOutput(base_ref, own_two_ref, other_two_ref, output_ref, rest[: LateOutput.COUNT])
    staging = rest[LateOutput.COUNT :]
    seq, tp = lax.axis_index("seq"), lax.axis_index("tp")
    level, side = seq // 2, seq % 2
    rows, width = grad_ref.shape
    heads = width // DH
    partner = (2 * level + 1 - side, tp)
    lane_head = head_of_lane(width)
    head_mask = head_masks(width)
    chunk = rows // 2
    barrier, greetings = greet(levels, True)

    def block_of(blocks_ref, from_level, place):
        if not staging:
            return blocks_ref.at[from_level]
        copy = pltpu.make_async_copy(blocks_ref.at[from_level], staging[place], staging[3])
        copy.start()
        copy.wait()
        return staging[place]

    own_query_ref = block_of(query_col_ref, level, 0)
    doc_first = doc_row_ref[0:1, 0:1]
    last = (level == levels - 1) & (side == 1)

    def prepare(index, unused):
        here = pl.ds(pl.multiple_of(index * chunk, chunk), chunk)
        grad = grad_ref[here, :]
        product = grad.astype(jnp.float32) * attended_ref[here, :]
        far = jnp.where(last & (doc_col_ref[here, :] != doc_first), -NEGATIVE, 0.0)
        lses = [lse_ref[here, head : head + 1] for head in range(heads)]
        deltas = [
            jnp.sum(jnp.where(lane_head == head, product, 0.0), axis=1, keepdims=True)
            for head in range(heads)
        ]
        own_ref[here, :] = with_stats(grad, lses + deltas)
        grad_col_ref[level, here, :] = with_stats(grad, [lse + far for lse in lses] + deltas)
        for head in range(heads):
            stat_ref[head, here, :] = lses[head]
            stat_ref[heads + head, here, :] = lses[head] + far
            stat_ref[2 * heads + head, here, :] = deltas[head]
        return unused

    lax.fori_loop(0, rows // chunk, prepare, 0)
    pl.semaphore_wait(barrier, greetings)

    def col_copy(from_level, to_level):
        return pltpu.make_async_remote_copy(
            grad_col_ref.at[from_level],
            grad_col_ref.at[from_level],
            col_send.at[to_level],
            col_recv.at[from_level],
            device_id=(2 * to_level + side, tp),
            device_id_type=MESH_ID,
        )

    def oth_copy(from_level):
        return pltpu.make_async_remote_copy(
            grad_col_ref.at[from_level],
            grad_oth_ref.at[from_level],
            oth_send.at[from_level],
            oth_recv.at[from_level],
            device_id=partner,
            device_id_type=MESH_ID,
        )

    @pl.when(side == 1)
    def _():
        oth_copy(level).start()

    def send_down(step, unused):
        col_copy(level, level - step).start()
        return unused

    lax.fori_loop(1, level + 1, send_down, 0)
    late.start()
    for scatter in scatters:
        scatter.start()

    mem_acc_ref[...] = jnp.zeros(mem_acc_ref.shape, jnp.float32)
    pull_ref[...] = jnp.zeros(pull_ref.shape, jnp.float32)

    def memory_back(index, unused):
        here = pl.ds(pl.multiple_of(index * chunk, chunk), chunk)
        query = own_query_ref[here, :].astype(jnp.float32)
        grad = grad_ref[here, :]
        val_parts, mu_pulls, sigma_pulls = [], [], []
        for head in range(heads):
            place = memory_place(query, spot_row_ref[0:2, :], lane_head == head)
            slope = place.gap / place.spread
            square = place.gap * slope
            density = place.height * jnp.exp(-0.5 * square)
            val_parts.append(dot_columns(density.astype(jnp.bfloat16), grad))
            weighed = dot_rows(grad * head_mask[head], mem_ref[:, width:]) * density
            to_centre = -jnp.sum(weighed * slope, axis=1, keepdims=True)
            to_spread = 0.5 * jnp.sum(weighed * (square - 1.0), axis=1, keepdims=True) / place.spread
            mu_pulls.append(to_centre * place.centre * (1.0 - place.centre))
            sigma_pulls.append(to_spread * SPREAD / (1.0 + jnp.exp(-place.loose)))
        mu_pull, sigma_pull = pick_heads(mu_pulls, lane_head), pick_heads(sigma_pulls, lane_head)
        dq_ref[here, :] = mu_pull * spot_row_ref[0:1, :] + sigma_pull * spot_row_ref[1:2, :]
        mem_acc_ref[...] += pick_heads(val_parts, lane_head)
        pull_ref[0:1, :] += column_sum(mu_pull * query)
        pull_ref[1:2, :] += column_sum(sigma_pull * query)
        return unused

    lax.fori_loop(0, rows // chunk, memory_back, 0)
    by_head = lax.broadcasted_iota(jnp.int32, (8, 1), 0) == lane_head
    pulls = [jnp.where(by_head, pull_ref[i : i + 1, :], 0.0) for i in range(2)]
    for index in range(2):
        spot_grad_ref[8 * index : 8 * index + 8, :] = sum(
            dot_rows(third, mem_ref[:, :width]) for third in thirds(pulls[index])
        )
    key_grad = dot_columns(
        spot_ref[...].astype(jnp.bfloat16), jnp.concatenate(pulls, axis=0).astype(jnp.bfloat16)
    )
    memory_grad = jnp.concatenate([key_grad, mem_acc_ref[...]], axis=1).astype(jnp.bfloat16)
    for slot in range(4):
        weight_grad_ref[slot * width : (slot + 1) * width, :] = jnp.concatenate(
            [jnp.zeros((width, width), jnp.float32), dot_columns(coeff_ref[slot], memory_grad)], axis=1
        ).astype(weight_grad_ref.dtype)

    dk_ref[...] = jnp.zeros(dk_ref.shape, jnp.float32)
    dv_ref[...] = jnp.zeros(dv_ref.shape, jnp.float32)

    def query_fold(kv_ref, from_level, own):
        block_ref = block_of(kv_ref, from_level, 2)
        if own:
            key_mask = None
        else:
            mask_rows = block_ref[rows:, :].astype(jnp.float32)
            key_mask = jnp.concatenate(
                [mask_rows[0:1, : rows // 2], mask_rows[1:2, : rows // 2]], axis=1
            )

        def part(index, unused):
            here = pl.ds(pl.multiple_of(index * chunk, chunk), chunk)
            query = own_query_ref[here, :]
            grad = grad_ref[here, :]
            keys = block_ref[:rows, :width]
            vals = block_ref[:rows, width:]
            if own:
                q_pos = index * chunk + lax.broadcasted_iota(jnp.int32, (chunk, rows), 0)
                k_pos = lax.broadcasted_iota(jnp.int32, (chunk, rows), 1)
                visible = (q_pos >= k_pos) & (doc_col_ref[here, :] == doc_row_ref[0:1, :])
            products = []
            for head in range(heads):
                scores = dot_rows(query * head_mask[head], keys)
                if own:
                    scores = jnp.where(visible, scores, NEGATIVE)
                    lse = stat_ref[head, here, :]
                else:
                    scores = scores + key_mask
                    lse = stat_ref[heads + head, here, :]
                probs = jnp.exp(scores - lse)
                pull = dot_rows(grad * head_mask[head], vals) - stat_ref[2 * heads + head, here, :]
                products.append(dot_plain((probs * pull).astype(jnp.bfloat16), keys))
            dq_ref[here, :] = dq_ref[here, :] + pick_heads(products, lane_head)
            return unused

        lax.fori_loop(0, rows // chunk, part, 0)

    query_fold(kv_col_ref, level, True)

    @pl.when(side == 1)
    def _():
        query_fold(kv_oth_ref, level, False)

    def earlier(from_level, unused):
        query_fold(kv_col_ref, from_level, False)
        query_fold(kv_oth_ref, from_level, False)
        return unused

    lax.fori_loop(0, level, earlier, 0)
    late.middle()
    for scatter in scatters:
        scatter.middle()

    own_block_ref = block_of(kv_col_ref, level, 2)

    def key_fold(query_ref, grads_ref, from_level, own):
        query_block_ref = own_query_ref if own else block_of(query_ref, from_level, 1)

        def part(index, unused):
            here = pl.ds(pl.multiple_of(index * chunk, chunk), chunk)
            keys = own_block_ref[here, :width]
            vals = own_block_ref[here, width:]
            if own:
                query = query_block_ref[...]
                extended = own_ref[...]
                k_pos = index * chunk + lax.broadcasted_iota(jnp.int32, (chunk, rows), 0)
                q_pos = lax.broadcasted_iota(jnp.int32, (chunk, rows), 1)
                visible = (q_pos >= k_pos) & (doc_col_ref[here, :] == doc_row_ref[0:1, :])
            else:
                query = query_block_ref[...]
                extended = grads_ref[from_level]
            grad = extended[:, :width]
            stats = stat_rows(extended, width, 8)
            key_parts, val_parts = [], []
            for head in range(heads):
                scores = dot_rows(keys * head_mask[head], query)
                if own:
                    scores = jnp.where(visible, scores, NEGATIVE)
                probs = jnp.exp(scores - stats[head : head + 1, :])
                val_parts.append(dot_plain(probs.astype(jnp.bfloat16), grad))
                pull = dot_rows(vals * head_mask[head], grad) - stats[heads + head : heads + head + 1, :]
                key_parts.append(dot_plain((probs * pull).astype(jnp.bfloat16), query))
            dk_ref[here, :] = dk_ref[here, :] + pick_heads(key_parts, lane_head)
            dv_ref[here, :] = dv_ref[here, :] + pick_heads(val_parts, lane_head)
            return unused

        lax.fori_loop(0, rows // chunk, part, 0)

    @pl.when(side == 0)
    def _():
        oth_copy(level).wait_recv()
        key_fold(query_oth_ref, grad_oth_ref, level, False)

    def later(step, unused):
        from_level = level + step
        col_copy(from_level, level).wait_recv()
        oth_copy(from_level).start()
        key_fold(query_col_ref, grad_col_ref, from_level, False)
        oth_copy(from_level).wait_recv()
        key_fold(query_oth_ref, grad_oth_ref, from_level, False)
        return unused

    lax.fori_loop(1, levels - level, later, 0)
    late.late()
    reaches = doc_col_ref[...] >= (seq + 1) * rows
    dk_ref[...] = jnp.where(reaches, dk_ref[...], 0.0)
    dv_ref[...] = jnp.where(reaches, dv_ref[...], 0.0)
    key_fold(None, None, level, True)
    grads_ref[...] = jnp.concatenate(
        [dq_ref[...] * (DH**-0.5), dk_ref[...], dv_ref[...]], axis=1
    ).astype(jnp.bfloat16)
    bias_grad_ref[...] = jnp.broadcast_to(
        column_sum(grads_ref[...].astype(jnp.float32)), bias_grad_ref.shape
    )

    def weights(index, unused):
        here = pl.ds(pl.multiple_of(index * 256, 256), 256)
        weight_grad_ref[here, :] = (
            weight_grad_ref[here, :].astype(jnp.float32) + dot_columns(normed_ref[:, here], grads_ref[...])
        ).astype(weight_grad_ref.dtype)
        return unused

    lax.fori_loop(0, D // 256, weights, 0)
    late.finish()
    for scatter, share_ref in zip(scatters, (proj_share_ref, fc_share_ref, out_share_ref)):
        scatter.finish(share_ref)

    @pl.when(side == 1)
    def _():
        oth_copy(level).wait_send()

    def sent_down(step, unused):
        col_copy(level, level - step).wait_send()
        return unused

    lax.fori_loop(1, level + 1, sent_down, 0)

    def sent_on(step, unused):
        oth_copy(level + step).wait_send()
        return unused

    lax.fori_loop(1, levels - level, sent_on, 0)


def attention_backward(
    levels,
    grad,
    attended,
    lse,
    query_col,
    query_oth,
    kv_col,
    kv_oth,
    doc_ids,
    blocks,
    base,
    own_two,
    other_two,
    normed,
    coeff,
    memory,
    spot_rows,
    spots,
):
    rows, width = grad.shape
    heads = width // DH
    vmem = pl.BlockSpec(memory_space=pltpu.VMEM)
    dma = pltpu.SemaphoreType.DMA
    staged = levels > 8
    far = pl.BlockSpec(memory_space=pl.ANY) if staged else vmem
    staging = []
    if staged:
        staging = [pltpu.VMEM(a.shape[1:], a.dtype) for a in (query_col, query_col, kv_col)] + [dma(())]
    return pl.pallas_call(
        functools.partial(backward_kernel, levels),
        out_shape=(
            jax.ShapeDtypeStruct((rows, 3 * width), jnp.bfloat16),
            jax.ShapeDtypeStruct((D, 3 * width), jnp.float32),
            jax.ShapeDtypeStruct((8, 3 * width), jnp.float32),
            jax.ShapeDtypeStruct((16, NB), jnp.float32),
            *(jax.ShapeDtypeStruct(block.shape[1:], jnp.float32) for block in blocks),
            jax.ShapeDtypeStruct((rows, D), jnp.bfloat16),
        ),
        in_specs=[vmem] * 3 + [far] * 4 + [vmem] * 13,
        out_specs=(vmem,) * 8,
        scratch_shapes=[
            pltpu.VMEM((rows, width), jnp.float32),
            pltpu.VMEM((rows, width), jnp.float32),
            pltpu.VMEM((rows, width), jnp.float32),
            pltpu.VMEM((NB, width), jnp.float32),
            pltpu.VMEM((8, width), jnp.float32),
            pltpu.VMEM((rows, LANES_OUT), jnp.bfloat16),
            pltpu.VMEM((levels, rows, LANES_OUT), jnp.bfloat16),
            pltpu.VMEM((levels, rows, LANES_OUT), jnp.bfloat16),
            pltpu.VMEM((3 * heads, rows, 1), jnp.float32),
            dma((levels,)),
            dma((levels,)),
            dma((levels,)),
            dma((levels,)),
            *(item for block in blocks for item in Scatter.scratch(levels, *block.shape[1:])),
            *LateOutput.scratch(rows // 2, D),
            *staging,
        ],
        name="attention_backward",
        compiler_params=pltpu.CompilerParams(
            collective_id=2, has_side_effects=True, vmem_limit_bytes=VMEM_LIMIT
        ),
    )(
        grad,
        attended,
        lse,
        query_col,
        query_oth,
        kv_col,
        kv_oth,
        doc_ids[:, None],
        doc_ids[None, :],
        *blocks,
        base,
        own_two,
        other_two,
        normed,
        coeff,
        memory,
        spot_rows,
        spots,
    )


def column_copy(block_ref, from_level, landing_ref, send_sem, recv_sem, to_level):
    seq, tp = lax.axis_index("seq"), lax.axis_index("tp")
    return pltpu.make_async_remote_copy(
        block_ref,
        landing_ref.at[from_level],
        send_sem.at[to_level],
        recv_sem.at[from_level],
        device_id=(2 * to_level + seq % 2, tp),
        device_id_type=MESH_ID,
    )


class Scatter:
    def __init__(self, levels, blocks, plane_in, plane_sum, column_in, sems):
        self.levels, self.blocks = levels, blocks
        self.plane_in, self.plane_sum, self.column_in = plane_in, plane_sum, column_in
        self.plane_send, self.plane_recv, self.column_send, self.column_recv = sems
        seq, tp = lax.axis_index("seq"), lax.axis_index("tp")
        self.level, self.side, self.tp = seq // 2, seq % 2, tp

    def plane_copy(self, to_level):
        return pltpu.make_async_remote_copy(
            self.blocks.at[2 * to_level + 1 - self.side],
            self.plane_in.at[to_level],
            self.plane_send.at[to_level],
            self.plane_recv.at[to_level],
            device_id=(2 * self.level + 1 - self.side, self.tp),
            device_id_type=MESH_ID,
        )

    def swap_copy(self, from_level, to_level):
        return column_copy(
            self.plane_sum.at[to_level], from_level, self.column_in, self.column_send, self.column_recv, to_level
        )

    def loop(self, first, body):
        def one(step, unused):
            body(lax.rem(self.level + step, self.levels))
            return unused

        lax.fori_loop(first, self.levels, one, 0)

    def start(self):
        self.loop(0, lambda other: self.plane_copy(other).start())

    def middle(self):
        def one(other):
            self.plane_copy(other).wait_recv()
            total = self.blocks[2 * other + self.side].astype(jnp.float32) + self.plane_in[other].astype(
                jnp.float32
            )
            self.plane_sum[other] = total.astype(jnp.bfloat16)
            self.swap_copy(self.level, other).start()

        self.loop(1, one)

    def finish(self, out_ref):
        self.plane_copy(self.level).wait_recv()
        out_ref[...] = self.blocks[2 * self.level + self.side].astype(jnp.float32) + self.plane_in[
            self.level
        ].astype(jnp.float32)

        def one(other):
            self.swap_copy(other, self.level).wait_recv()
            out_ref[...] += self.column_in[other].astype(jnp.float32)

        self.loop(1, one)
        self.loop(0, lambda other: self.plane_copy(other).wait_send())
        self.loop(1, lambda other: self.swap_copy(self.level, other).wait_send())

    @staticmethod
    def scratch(levels, rows, width):
        buffer = pltpu.VMEM((levels, rows, width), jnp.bfloat16)
        return [buffer] * 3 + [pltpu.SemaphoreType.DMA((levels,))] * 4


class SmallSum:
    def __init__(self, levels, small, plane_in, column_in, sems):
        self.levels, self.small, self.plane_in, self.column_in = levels, small, plane_in, column_in
        self.plane_sem, self.column_send, self.column_recv = sems
        seq, tp = lax.axis_index("seq"), lax.axis_index("tp")
        self.level, self.side, self.tp = seq // 2, seq % 2, tp

    def plane_copy(self):
        return pltpu.make_async_remote_copy(
            self.small,
            self.plane_in,
            self.plane_sem.at[0],
            self.plane_sem.at[1],
            device_id=(2 * self.level + 1 - self.side, self.tp),
            device_id_type=MESH_ID,
        )

    def swap_copy(self, from_level, to_level):
        return column_copy(
            self.column_in.at[from_level], from_level, self.column_in, self.column_send, self.column_recv, to_level
        )

    def loop(self, body):
        def one(step, unused):
            body(lax.rem(self.level + step, self.levels))
            return unused

        lax.fori_loop(1, self.levels, one, 0)

    def start(self):
        self.plane_copy().start()

    def middle(self):
        self.plane_copy().wait()
        self.column_in[self.level] = self.small[...] + self.plane_in[...]
        self.loop(lambda other: self.swap_copy(self.level, other).start())

    def finish(self, out_ref):
        self.loop(lambda other: self.swap_copy(other, self.level).wait_recv())
        self.loop(lambda other: self.swap_copy(self.level, other).wait_send())
        out_ref[...] = self.column_in[0]

        def one(other, unused):
            out_ref[...] += self.column_in[other]
            return unused

        lax.fori_loop(1, self.levels, one, 0)

    @staticmethod
    def scratch(levels, shape):
        dma = pltpu.SemaphoreType.DMA
        return [
            pltpu.VMEM(shape, jnp.float32),
            pltpu.VMEM((levels,) + shape, jnp.float32),
            dma((2,)),
            dma((levels,)),
            dma((levels,)),
        ]


def tp_partner(kind):
    seq, tp = lax.axis_index("seq"), lax.axis_index("tp")
    if kind == "core":
        return (seq, tp + 1 - 2 * (tp % 2))
    return (seq, lax.rem(tp + 2, 4))


def greet_tp():
    barrier = pltpu.get_barrier_semaphore()
    for kind in ("core", "chip"):
        pl.semaphore_signal(barrier, inc=1, device_id=tp_partner(kind), device_id_type=MESH_ID)
    return barrier, 2


def swap_with(kind, source, target, sems, index):
    send, recv = sems
    return pltpu.make_async_remote_copy(
        source, target, send.at[index], recv.at[index], device_id=tp_partner(kind), device_id_type=MESH_ID
    )


class TpSum:
    def __init__(self, core_out, core_in, chip_out, chip_in, sems):
        self.core_out, self.core_in, self.chip_out, self.chip_in = core_out, core_in, chip_out, chip_in
        self.core_sems, self.chip_sems = sems[:2], sems[2:]

    def core_copy(self, part):
        return swap_with("core", self.core_out.at[part], self.core_in.at[part], self.core_sems, part)

    def chip_copy(self, part):
        return swap_with("chip", self.chip_out.at[part], self.chip_in.at[part], self.chip_sems, part)

    def start(self, part, for_other_core):
        self.core_out[part] = for_other_core.astype(jnp.bfloat16)
        self.core_copy(part).start()

    def middle(self, part, own):
        self.core_copy(part).wait()
        self.chip_out[part] = (own + self.core_in[part].astype(jnp.float32)).astype(jnp.bfloat16)
        self.chip_copy(part).start()

    def result(self, part):
        self.chip_copy(part).wait()
        return self.chip_out[part].astype(jnp.float32) + self.chip_in[part].astype(jnp.float32)

    @staticmethod
    def scratch(parts, rows, width):
        buffer = pltpu.VMEM((parts, rows, width), jnp.bfloat16)
        return [buffer] * 4 + [pltpu.SemaphoreType.DMA((parts,))] * 4

    COUNT = 8


class RowShare:
    def __init__(self, whole, rows, sems):
        self.whole, self.rows, self.sems = whole, rows, sems

    def copy(self, part, start):
        here = self.whole.at[pl.ds(pl.multiple_of(start, self.rows), self.rows), :]
        return swap_with("core", here, here, self.sems, part)


def normalize(v):
    centred = v - jnp.mean(v, axis=1, keepdims=True)
    scale = lax.rsqrt(jnp.mean(centred * centred, axis=1, keepdims=True) + EPS)
    return centred * scale, scale


def norm_back(grad, nhat, scale, gain):
    inner = grad * gain
    return (
        inner
        - jnp.mean(inner, axis=1, keepdims=True)
        - nhat * jnp.mean(inner * nhat, axis=1, keepdims=True)
    ) * scale


def gelu_and_slope(f):
    root = (2.0 / np.pi) ** 0.5
    square = f * f
    bend = jnp.tanh(root * f * (1.0 + 0.044715 * square))
    half = 0.5 * (1.0 + bend)
    slope = half + 0.5 * f * (1.0 - bend * bend) * (root * (1.0 + 3.0 * 0.044715 * square))
    return f * half, slope


def dot_columns(left, right):
    return lax.dot_general(left, right, (((0,), (0,)), ((), ())), preferred_element_type=jnp.float32)


def column_sum(v):
    return jnp.sum(v, axis=0, keepdims=True)


FEED_PARTS = 2


def feed_kernel(
    heads_ref,
    tok_ref,
    cot_ref,
    out_w_ref,
    fc_w_ref,
    proj_w_ref,
    vec_ref,
    proj_grad_ref,
    fc_grad_ref,
    out_grad_ref,
    head_grad_ref,
    mid_grad_ref,
    base_ref,
    own_two_ref,
    other_two_ref,
    sums_ref,
    c_ref,
    e1_ref,
    u_ref,
    ef_ref,
    pull_ref,
    h1_ref,
    own_ref,
    fold_in_ref,
    *sems,
):
    parts = FEED_PARTS
    rows = tok_ref.shape[0]
    half = rows // 2
    size = half // parts
    tp = lax.axis_index("tp")
    core = tp % 2
    first = TpSum(*sems[:4], sems[4 : TpSum.COUNT])
    second = TpSum(*sems[TpSum.COUNT : TpSum.COUNT + 4], sems[TpSum.COUNT + 4 : 2 * TpSum.COUNT])
    sems = sems[2 * TpSum.COUNT :]
    c_share = RowShare(c_ref, size, sems[0:2])
    e_share = RowShare(e1_ref, size, sems[2:4])
    fold_sems = sems[4:6]
    barrier, greetings = greet_tp()
    gain, offset, out_b, fc_b, proj_b = (vec_ref[i : i + 1, :] for i in range(5))

    def span(start, count=size):
        return pl.ds(pl.multiple_of(start, size), count)

    def mine(part):
        return core * half + part * size

    def theirs(part):
        return (1 - core) * half + part * size

    pl.semaphore_wait(barrier, greetings)
    for part in range(parts):
        first.start(part, dot_plain(heads_ref[span(theirs(part)), :], out_w_ref[...]))
        own_ref[span(part * size), :] = dot_plain(heads_ref[span(mine(part)), :], out_w_ref[...])
    for part in range(parts):
        first.middle(part, own_ref[span(part * size), :])

    def early(index, unused):
        here = span(index * size)
        pull_ref[here, :] = dot_rows(cot_ref[here, :], proj_w_ref[...])
        return unused

    lax.fori_loop(0, rows // size, early, 0)

    def feed(start):
        here = span(start)
        f = dot_plain(c_ref[here, :], fc_w_ref[...]) + fc_b
        u, slope = gelu_and_slope(f)
        u_ref[here, :] = u.astype(jnp.bfloat16)
        ef = (pull_ref[here, :] * slope).astype(jnp.bfloat16)
        ef_ref[here, :] = ef
        return dot_rows(ef, fc_w_ref[...])

    for part in range(parts):
        total = first.result(part) + out_b
        h1 = tok_ref[span(mine(part)), :].astype(jnp.float32) + total
        h1_ref[span(part * size), :] = h1
        nhat, scale = normalize(h1)
        c_ref[span(mine(part)), :] = (nhat * gain + offset).astype(jnp.bfloat16)
        c_share.copy(part, mine(part)).start()
        own_ref[span(part * size), :] = feed(mine(part))
        c_share.copy(part, theirs(part)).wait_recv()
        second.start(part, feed(theirs(part)))
        other_two_ref[span(part * size), :] = dot_plain(u_ref[span(theirs(part)), :], proj_w_ref[...]).astype(
            jnp.bfloat16
        )
        own_two_ref[span(part * size), :] = dot_plain(u_ref[span(mine(part)), :], proj_w_ref[...])
        second.middle(part, own_ref[span(part * size), :])

    base_ref[...] = h1_ref[...] + proj_b
    block = 256

    def weights(index, unused):
        here = pl.ds(pl.multiple_of(index * block, block), block)
        proj_grad_ref[here, :] = dot_columns(cot_ref[:, here], u_ref[...]).astype(jnp.bfloat16)
        fc_grad_ref[here, :] = dot_columns(c_ref[:, here], ef_ref[...]).astype(jnp.bfloat16)
        return unused

    lax.fori_loop(0, D // block, weights, 0)
    fc_sum = column_sum(ef_ref[...].astype(jnp.float32))

    gain_sum = jnp.zeros((1, D), jnp.float32)
    offset_sum = jnp.zeros((1, D), jnp.float32)
    out_sum = jnp.zeros((1, D), jnp.float32)
    for part in range(parts):
        grad = second.result(part)
        nhat, scale = normalize(h1_ref[span(part * size), :])
        gain_sum = gain_sum + column_sum(grad * nhat)
        offset_sum = offset_sum + column_sum(grad)
        mid = cot_ref[span(mine(part)), :].astype(jnp.float32) + norm_back(grad, nhat, scale, gain)
        mid_grad_ref[span(part * size), :] = mid
        e1 = mid.astype(jnp.bfloat16)
        out_sum = out_sum + column_sum(e1.astype(jnp.float32))
        e1_ref[span(mine(part)), :] = e1
        e_share.copy(part, mine(part)).start()
        head_grad_ref[span(mine(part)), :] = dot_rows(e1, out_w_ref[...]).astype(jnp.bfloat16)
    row = lax.broadcasted_iota(jnp.int32, (8, 1), 0)
    sums_ref[...] = jnp.where(row == 0, gain_sum, jnp.where(row == 1, offset_sum, out_sum))
    fold_copy = swap_with("core", sums_ref, fold_in_ref, fold_sems, 0)
    fold_copy.start()
    for part in range(parts):
        e_share.copy(part, theirs(part)).wait_recv()
        head_grad_ref[span(theirs(part)), :] = dot_rows(e1_ref[span(theirs(part)), :], out_w_ref[...]).astype(
            jnp.bfloat16
        )

    def out_weights(index, unused):
        here = pl.ds(pl.multiple_of(index * block, block), block)
        out_grad_ref[here, :] = dot_columns(e1_ref[:, here], heads_ref[...]).astype(jnp.bfloat16)
        return unused

    lax.fori_loop(0, D // block, out_weights, 0)
    fold_copy.wait()
    sums_ref[...] = jnp.where(row == 3, fc_sum, sums_ref[...] + fold_in_ref[...])
    for part in range(parts):
        c_share.copy(part, mine(part)).wait_send()
        e_share.copy(part, mine(part)).wait_send()


def feed_forward(heads, tokens, cotangent, out_w, fc_w, proj_w, vectors):
    rows, width = heads.shape
    half = rows // 2
    hidden = fc_w.shape[1]
    parts, size = FEED_PARTS, half // FEED_PARTS
    vmem = pl.BlockSpec(memory_space=pltpu.VMEM)
    dma = pltpu.SemaphoreType.DMA
    bf, fl = jnp.bfloat16, jnp.float32
    shape = jax.ShapeDtypeStruct
    return pl.pallas_call(
        feed_kernel,
        out_shape=(
            shape((D, hidden), bf),
            shape((D, hidden), bf),
            shape((D, width), bf),
            shape((rows, width), bf),
            shape((half, D), fl),
            shape((half, D), fl),
            shape((half, D), fl),
            shape((half, D), bf),
            shape((8, D), fl),
        ),
        in_specs=[vmem] * 7,
        out_specs=(vmem,) * 9,
        scratch_shapes=[
            pltpu.VMEM((rows, D), bf),
            pltpu.VMEM((rows, D), bf),
            pltpu.VMEM((rows, hidden), bf),
            pltpu.VMEM((rows, hidden), bf),
            pltpu.VMEM((rows, hidden), fl),
            pltpu.VMEM((half, D), fl),
            pltpu.VMEM((half, D), fl),
            pltpu.VMEM((8, D), fl),
            *TpSum.scratch(parts, size, D),
            *TpSum.scratch(parts, size, D),
            dma((parts,)),
            dma((parts,)),
            dma((parts,)),
            dma((parts,)),
            dma((1,)),
            dma((1,)),
        ],
        name="feed_forward",
        compiler_params=pltpu.CompilerParams(
            collective_id=4, has_side_effects=True, vmem_limit_bytes=VMEM_LIMIT
        ),
    )(heads, tokens, cotangent, out_w, fc_w, proj_w, vectors)


class LateOutput:
    def __init__(self, base, own, other, whole, sems):
        self.base, self.own, self.other, self.whole = base, own, other, whole
        self.half = own.shape[0]
        self.core_in, self.chip_out, self.chip_in = sems[:3]
        self.core_sems, self.chip_sems, self.share_sems = sems[3:5], sems[5:7], sems[7:9]
        self.share = RowShare(whole, self.half, self.share_sems)
        self.core = lax.axis_index("tp") % 2

    COUNT = 9

    def core_copy(self):
        return swap_with("core", self.other, self.core_in, self.core_sems, 0)

    def chip_copy(self):
        return swap_with("chip", self.chip_out, self.chip_in, self.chip_sems, 0)

    def start(self):
        self.core_copy().start()

    def middle(self):
        self.core_copy().wait()
        self.chip_out[...] = (self.own[...] + self.core_in[...].astype(jnp.float32)).astype(jnp.bfloat16)
        self.chip_copy().start()

    def late(self):
        self.chip_copy().wait()
        total = self.chip_out[...].astype(jnp.float32) + self.chip_in[...].astype(jnp.float32)
        here = pl.ds(pl.multiple_of(self.core * self.half, self.half), self.half)
        self.whole[here, :] = (self.base[...] + total).astype(jnp.bfloat16)
        self.share.copy(0, self.core * self.half).start()

    def finish(self):
        self.share.copy(0, (1 - self.core) * self.half).wait_recv()
        self.share.copy(0, self.core * self.half).wait_send()

    @staticmethod
    def scratch(half, width):
        buffer = pltpu.VMEM((half, width), jnp.bfloat16)
        return [buffer] * 3 + [pltpu.SemaphoreType.DMA((1,))] * 6


def finish_kernel(
    levels,
    grads_ref,
    weight_ref,
    tok_ref,
    mid_grad_ref,
    norm_ref,
    blocks_ref,
    small_in_ref,
    tokens_out_ref,
    share_ref,
    small_out_ref,
    own_ref,
    small_ref,
    fold_ref,
    fold_in_ref,
    *rest,
):
    parts = FEED_PARTS
    rows = tok_ref.shape[0]
    half = rows // 2
    size = half // parts
    core = lax.axis_index("tp") % 2
    total = TpSum(*rest[:4], rest[4 : TpSum.COUNT])
    rest = rest[TpSum.COUNT :]
    scatter = Scatter(levels, blocks_ref, *rest[:3], rest[3:7])
    rest = rest[7:]
    small = SmallSum(levels, small_ref, rest[0], rest[1], rest[2:5])
    rest = rest[5:]
    share = RowShare(tokens_out_ref, size, rest[0:2])
    fold_sems = rest[2:4]
    barrier, greetings = greet(levels, True)
    gain = norm_ref[0:1, :]

    def span(start, count=size):
        return pl.ds(pl.multiple_of(start, size), count)

    def mine(part):
        return core * half + part * size

    def theirs(part):
        return (1 - core) * half + part * size

    pl.semaphore_wait(barrier, greetings)
    scatter.start()
    for part in range(parts):
        total.start(part, dot_rows(grads_ref[span(theirs(part)), :], weight_ref[...]))
        own_ref[span(part * size), :] = dot_rows(grads_ref[span(mine(part)), :], weight_ref[...])
    for part in range(parts):
        total.middle(part, own_ref[span(part * size), :])
    scatter.middle()
    gain_sum = jnp.zeros((1, D), jnp.float32)
    offset_sum = jnp.zeros((1, D), jnp.float32)
    for part in range(parts):
        grad = total.result(part)
        nhat, scale = normalize(tok_ref[span(mine(part)), :].astype(jnp.float32))
        gain_sum = gain_sum + column_sum(grad * nhat)
        offset_sum = offset_sum + column_sum(grad)
        out = mid_grad_ref[span(part * size), :] + norm_back(grad, nhat, scale, gain)
        tokens_out_ref[span(mine(part)), :] = out.astype(jnp.bfloat16)
        share.copy(part, mine(part)).start()
    row = lax.broadcasted_iota(jnp.int32, (8, 1), 0)
    fold_ref[...] = jnp.where(row == 0, gain_sum, jnp.where(row == 1, offset_sum, 0.0))
    fold_copy = swap_with("core", fold_ref, fold_in_ref, fold_sems, 0)
    fold_copy.start()
    fold_copy.wait()
    small_ref[8:, :] = small_in_ref[8:, :]
    small_ref[:8, :] = small_in_ref[:8, :] + (fold_ref[...] + fold_in_ref[...])
    small.start()
    small.middle()
    scatter.finish(share_ref)
    small.finish(small_out_ref)
    for part in range(parts):
        share.copy(part, theirs(part)).wait_recv()
        share.copy(part, mine(part)).wait_send()


def finish_layer(levels, grads, weight, tokens, mid_grad, norm, blocks, small):
    rows = tokens.shape[0]
    half = rows // 2
    parts, size = FEED_PARTS, half // FEED_PARTS
    vmem = pl.BlockSpec(memory_space=pltpu.VMEM)
    dma = pltpu.SemaphoreType.DMA
    shape = jax.ShapeDtypeStruct
    return pl.pallas_call(
        functools.partial(finish_kernel, levels),
        out_shape=(
            shape((rows, D), jnp.bfloat16),
            shape(blocks.shape[1:], jnp.float32),
            shape(small.shape, jnp.float32),
        ),
        in_specs=[vmem] * 7,
        out_specs=(vmem,) * 3,
        scratch_shapes=[
            pltpu.VMEM((half, D), jnp.float32),
            pltpu.VMEM(small.shape, jnp.float32),
            pltpu.VMEM((8, D), jnp.float32),
            pltpu.VMEM((8, D), jnp.float32),
            *TpSum.scratch(parts, size, D),
            *Scatter.scratch(levels, *blocks.shape[1:]),
            *SmallSum.scratch(levels, small.shape),
            dma((parts,)),
            dma((parts,)),
            dma((1,)),
            dma((1,)),
        ],
        name="finish_layer",
        compiler_params=pltpu.CompilerParams(
            collective_id=3, has_side_effects=True, vmem_limit_bytes=VMEM_LIMIT
        ),
    )(grads, weight, tokens, mid_grad, norm, blocks, small)


def local(
    tokens,
    cotangent,
    past_states,
    doc_ids,
    cur_book,
    past_book,
    past_age,
    ln1_gain,
    ln1_bias,
    qkv_weight,
    qv_bias,
    out_weight,
    out_bias,
    ln2_gain,
    ln2_bias,
    fc_weight,
    fc_bias,
    proj_weight,
    proj_bias,
    mu_weight,
    sigma_weight,
):
    tok_rows = tokens.shape[0]
    heads_here = mu_weight.shape[0]
    head_cols = qkv_weight.shape[2]
    seq_count = lax.axis_size("seq")
    seq_index = lax.axis_index("seq")
    levels = seq_count // 2
    row_pad = ((0, 6), (0, 0))
    norm_rows = jnp.pad(jnp.stack([ln1_gain, ln1_bias]), row_pad)
    qkv_flat = qkv_weight.reshape(D, 3 * head_cols)
    bias_row = jnp.concatenate([qv_bias[0], jnp.zeros(head_cols, jnp.float32), qv_bias[1]])
    bias_rows = jnp.broadcast_to(bias_row[None], (8, 3 * head_cols))
    reaches = doc_ids >= (seq_index + 1) * tok_rows
    key_mask = jnp.where(reaches, 0.0, NEGATIVE).astype(jnp.bfloat16).reshape(2, tok_rows // 2)
    key_mask = jnp.pad(key_mask, ((0, 14), (0, 2 * head_cols - tok_rows // 2)))

    quarter = D // lax.axis_size("tp")
    columns = lax.dynamic_slice_in_dim(
        past_states, lax.axis_index("tp") * quarter, quarter, axis=1
    )
    half = SEG // 2
    marks = jnp.concatenate([past_book, past_age, jnp.zeros(14, jnp.int32)]).astype(jnp.bfloat16)
    past = jnp.concatenate(
        [
            jnp.concatenate([columns[:half], columns[half:]], axis=1),
            jnp.broadcast_to(marks[:, None], (16, 2 * quarter)),
        ]
    )
    book = jnp.broadcast_to(cur_book.astype(jnp.float32)[:, None], (8, 2 * quarter))
    spots = jnp.pad(jnp.stack([mu_weight, sigma_weight]), ((0, 0), (0, 8 - heads_here), (0, 0)))
    spots = spots.reshape(16, NB)
    table = jnp.asarray(np.stack(coefficient_tables(seq_count // BOOKS, NB, SEG), axis=1))

    normed_one, query_col, kv_col, attended, log_sum, heads_out, coeff, memory, spot_rows = (
        attention_forward(
            levels,
            tokens,
            norm_rows,
            qkv_flat,
            bias_rows,
            doc_ids,
            key_mask,
            past,
            book,
            spots,
            table,
        )
    )
    swap = [(index, index ^ 1) for index in range(seq_count)]
    query_oth = lax.ppermute(query_col, "seq", swap)
    kv_oth = lax.ppermute(kv_col, "seq", swap)

    vectors = jnp.pad(
        jnp.stack([ln2_gain, ln2_bias, out_bias, fc_bias, proj_bias]), ((0, 3), (0, 0))
    )
    proj_grad, fc_grad, out_grad, grad_heads, mid_grad, base, own_two, other_two, mid_sums = (
        feed_forward(heads_out, tokens, cotangent, out_weight, fc_weight, proj_weight, vectors)
    )
    grad_proj_b = jnp.sum(cotangent.astype(jnp.float32), axis=0)

    def shards(grad):
        return grad.astype(jnp.bfloat16).reshape(seq_count, D // seq_count, -1)

    grad_qkv, qkv_grad, bias_grad, spot_grad, proj_share, fc_share, out_share, output = (
        attention_backward(
            levels,
            grad_heads,
            attended,
            log_sum,
            query_col,
            query_oth,
            kv_col,
            kv_oth,
            doc_ids,
            [shards(proj_grad), shards(fc_grad), shards(out_grad)],
            base,
            own_two,
            other_two,
            normed_one,
            coeff,
            memory,
            spot_rows,
            spots,
        )
    )
    bias_sums = jnp.concatenate([bias_grad[0, :head_cols], bias_grad[0, 2 * head_cols :]])
    nothing = jnp.zeros((2, D), jnp.float32)
    small = jnp.concatenate(
        [
            nothing,
            mid_sums[:4],
            grad_proj_b[None],
            jnp.pad(bias_sums[None], ((0, 0), (0, D - 2 * head_cols))),
            spot_grad[:heads_here].reshape(2, D),
            spot_grad[8 : 8 + heads_here].reshape(2, D),
            nothing,
            nothing,
        ]
    )
    grad_tokens, qkv_share, small = finish_layer(
        levels, grad_qkv, qkv_flat, tokens, mid_grad, norm_rows, shards(qkv_grad), small
    )
    return (
        output,
        grad_tokens,
        qkv_share.reshape(-1, 3, head_cols),
        small[7, : 2 * head_cols].reshape(2, head_cols),
        out_share.T,
        small[4],
        fc_share,
        small[5],
        proj_share.T,
        small[6],
        small[0],
        small[1],
        small[2],
        small[3],
        small[8:10].reshape(heads_here, NB),
        small[10:12].reshape(heads_here, NB),
    )


def solution(mesh):
    in_specs = (
        P("seq", None),
        P("seq", None),
        P("seq", None),
        P("seq"),
        P("seq"),
        P("seq"),
        P("seq"),
        P(),
        P(),
        P(None, None, "tp"),
        P(None, "tp"),
        P("tp", None),
        P(),
        P(),
        P(),
        P(None, "tp"),
        P("tp"),
        P("tp", None),
        P(),
        P("tp", None),
        P("tp", None),
    )
    out_specs = (
        P("seq", None),
        P("seq", None),
        P("seq", None, "tp"),
        P(None, "tp"),
        P("tp", "seq"),
        P(),
        P("seq", "tp"),
        P("tp"),
        P("tp", "seq"),
        P(),
        P(),
        P(),
        P(),
        P(),
        P("tp", None),
        P("tp", None),
    )
    return jax.shard_map(local, mesh=mesh, in_specs=in_specs, out_specs=out_specs, check_vma=False)
```

profile of v0, /device:TPU:0, one launch (start us, length us, event | category | flops | bytes accessed | tf_op | source)
XLA Modules:
  0.0 259.7 jit_solution(6964237596860052967)
XLA Ops:
  0.6 0.0 copy-start.7
  2.0 0.8 fusion.4
  2.8 2.2 copy.48.weight_ref
  5.1 0.9 copy.49.doc_col_ref
  6.6 0.6 fusion.spot_ref
  7.3 0.6 select_maximum_fusion.1.norm_ref
  7.9 0.6 pad.21.key_mask_ref
  8.5 1.2 constant_dynamic-slice_fusion
  9.7 0.1 pad_maximum_fusion.2
  9.8 0.8 maximum_maximum_fusion.past_ref
  10.6 0.1 pad_maximum_fusion
  10.7 0.6 broadcast_in_dim.49.bias_ref
  11.3 0.6 broadcast_in_dim.56.book_ref
  11.9 66.0 %attention_forward.1 = (bf16[512,768]{1,0:T(8,128)(2,1)}, bf16[4,512,192]{2,1,0:T(8,128)(2,1)}, bf16[4,528,384]{2,1,0:T(8,128)(2,1)}, f32[512,192]{1,0:T(8,128)}...) custom-call(bf16[512,768]{1,0:T(8,128)(2,1)} %tok_ref.5, ...), custom_call_target="tpu_custom_call" | custom-call | tf_op jit(solution)/shard_map/attention_forward/pallas_call | solution.py:541
  77.9 0.0 copy-start.12
  77.9 0.0 copy-start.13
  78.0 0.0 copy-start.15
  78.0 0.0 copy-start.16
  78.0 0.6 collective-permute-start.1
  78.6 1.5 copy.50
  80.1 1.5 collective-permute-start
  81.7 0.6 pad.23.vec_ref
  82.3 30.5 %feed_forward.1 = (bf16[768,768]{1,0:T(8,128)(2,1)}, bf16[768,768]{1,0:T(8,128)(2,1)}, bf16[768,192]{1,0:T(8,128)(2,1)}, bf16[512,192]{1,0:T(8,128)(2,1)}, f32[2...) custom-call(bf16[512,192]{1,0:T(8,128)(2,1)} %get-tuple-element.45.h, ...), custom_call_target="tpu_custom_call" | custom-call | tf_op jit(solution)/shard_map/feed_forward/pallas_call | solution.py:1380
  112.9 0.7 slice.61
  113.6 0.1 convert_reduce_fusion
  113.8 19.2 %collective-permute-done = bf16[4,512,192]{1,2,0:T(8,128)(2,1)S(1)} collective-permute-done((bf16[4,512,192]{1,2,0:T(8,128)(2,1)S(1)}, bf16[4,512,192]{1,2,0:T(8,128)(2,1)S(1)}, u32[]{:S(2)}, u32[]{:S(2)}) %collective-permute-start) | collective-permute-done | bytes 786464 | tf_op jit(solution)/shard_map/ppermute | solution.py:1646
  132.9 1.3 copy.51.query_oth_ref
  134.2 1.2 copy-done.1
  135.4 78.9 %attention_backward.1 = (bf16[512,576]{1,0:T(8,128)(2,1)}, f32[768,576]{1,0:T(8,128)}, f32[8,576]{1,0:T(8,128)}, f32[16,512]{1,0:T(8,128)}, f32[96,768]{1,0:T(8,...) custom-call(bf16[512,192]{1,0:T(8,128)(2,1)} %get-tuple-element.46.grad_ref, ...), custom_call_target="tpu_custom_call" | custom-call | tf_op jit(solution)/shard_map/attention_backward/pallas_call | solution.py:942
  214.4 0.7 fusion.3
  215.1 0.1 pad_maximum_fusion.1
  215.2 0.7 fusion.2
  215.9 2.6 %convert_element_type.29 = bf16[768,576]{1,0:T(8,128)(2,1)} convert(f32[768,576]{1,0:T(8,128)} %get-tuple-element.64) | non-fusion elementwise | flops 442368 | bytes 2654208 | tf_op jit(solution)/shard_map/convert_element_type | solution.py:1658
  218.6 1.3 concatenate.35.small_in_ref
  219.9 28.8 %finish_layer.1 = (bf16[512,768]{1,0:T(8,128)(2,1)}, f32[96,576]{1,0:T(8,128)}, f32[16,768]{1,0:T(8,128)}) custom-call(bf16[512,576]{1,0:T(8,128)(2,1)} %get-tuple-element.62.grads_ref, bf16[768,576]{1,0:T(8,128)(2,1)} %copy.48.weight_ref, bf16[512,768]{1,0:T(8,128)(2,1)} %tok_ref.5, f32[256,768]{1,0:T(8,128)} %get-tuple-element.63.mid_grad_ref, ...), custom_call_target="tpu_custom_call" | custom-call | tf_op jit(solution)/shard_map/finish_layer/pallas_call | solution.py:1546
  248.7 1.7 slice_reduce_fusion
  250.4 0.8 fusion.1
  251.2 0.7 slice_reduce_fusion.7
  251.9 1.1 copy.54
  253.0 0.9 copy.55
  253.9 0.6 reshape.100
  254.5 0.6 reshape.99
  255.1 0.7 reshape_squeeze.3
  255.8 0.7 copy.56
  256.6 0.9 copy.64
  257.4 0.9 copy.65
  258.3 0.7 copy.66
  259.0 0.7 copy.67
  (48 shorter events, 0.2 us)
Async XLA Ops:
  0.6 4.4 %copy-start.7 = (s32[512]{0:T(512)S(1)}, s32[512]{0:T(512)}, u32[]{:S(2)}) copy-start(s32[512]{0:T(512)} %param.25) | copy-start | bytes 6148
  0.7 5.3 %copy-start.10 = (f32[768]{0:T(1024)S(1)}, f32[768]{0:T(1024)}, u32[]{:S(2)}) copy-start(f32[768]{0:T(1024)} %param.29) | copy-start | bytes 9220
  0.7 5.2 %copy-start.11 = (f32[768]{0:T(1024)S(1)}, f32[768]{0:T(1024)}, u32[]{:S(2)}) copy-start(f32[768]{0:T(1024)} %param.30) | copy-start | bytes 9220
  0.7 5.9 %copy-start.9 = (f32[3,512]{1,0:T(4,128)S(1)}, f32[3,512]{1,0:T(4,128)}, u32[]{:S(2)}) copy-start(f32[3,512]{1,0:T(4,128)} %param.41) | copy-start | bytes 18436
  0.7 5.9 %copy-start.8 = (f32[3,512]{1,0:T(4,128)S(1)}, f32[3,512]{1,0:T(4,128)}, u32[]{:S(2)}) copy-start(f32[3,512]{1,0:T(4,128)} %param.42) | copy-start | bytes 18436
  77.9 3.7 %copy-start.12 = (f32[768]{0:T(1024)S(1)}, f32[768]{0:T(1024)}, u32[]{:S(2)}) copy-start(f32[768]{0:T(1024)} %param.35) | copy-start | bytes 9220
  77.9 3.7 %copy-start.13 = (f32[768]{0:T(1024)S(1)}, f32[768]{0:T(1024)}, u32[]{:S(2)}) copy-start(f32[768]{0:T(1024)} %param.36) | copy-start | bytes 9220
  77.9 3.7 %copy-start.14 = (f32[768]{0:T(1024)S(1)}, f32[768]{0:T(1024)}, u32[]{:S(2)}) copy-start(f32[768]{0:T(1024)} %param.34) | copy-start | bytes 9220
  78.0 3.7 %copy-start.15 = (f32[768]{0:T(1024)S(1)}, f32[768]{0:T(1024)}, u32[]{:S(2)}) copy-start(f32[768]{0:T(1024)} %param.38) | copy-start | bytes 9220
  78.0 3.7 %copy-start.16 = (f32[768]{0:T(1024)S(1)}, f32[768]{0:T(1024)}, u32[]{:S(2)}) copy-start(f32[768]{0:T(1024)} %param.40) | copy-start | bytes 9220
  78.0 56.2 %collective-permute-start.1 = (bf16[4,528,384]{2,1,0:T(8,128)(2,1)}, bf16[4,528,384]{2,1,0:T(8,128)(2,1)S(1)}, u32[]{:S(2)}, u32[]{:S(2)}) collective-permute-start(bf16[4,528,384]{2,1,0:T(8,128)(2,1)} %get-tuple-element.50.kv_col_ref), channel_id=1, source_target_pairs={{0,4},{4,0},{8,12},{12,8},{16,20},{20,16},{24,28},{28,24},{1,5},{5... | collective-permute-start | bytes 4866056 | tf_op jit(solution)/shard_map/ppermute | solution.py:1647
  80.1 52.9 %collective-permute-start = (bf16[4,512,192]{1,2,0:T(8,128)(2,1)S(1)}, bf16[4,512,192]{1,2,0:T(8,128)(2,1)S(1)}, u32[]{:S(2)}, u32[]{:S(2)}) collective-permute-start(bf16[4,512,192]{1,2,0:T(8,128)(2,1)S(1)} %copy.50), channel_id=1, source_target_pairs={{0,4},{4,0},{8,12},{12,8},{16,20},{20,16},{24,28},{28,24},{1,5},{5... | collective-permute-start | bytes 2359304 | tf_op jit(solution)/shard_map/ppermute | solution.py:1646
  82.3 31.3 %copy-start = (bf16[512,768]{1,0:T(8,128)(2,1)S(1)}, bf16[512,768]{1,0:T(8,128)(2,1)}, u32[]{:S(2)}) copy-start(bf16[512,768]{1,0:T(8,128)(2,1)} %cot_ref.1) | copy-start | bytes 2359300
  134.2 1.2 copy-start.1
  219.9 36.0 %copy-start.6 = (f32[96,192]{1,0:T(8,128)S(1)}, f32[96,192]{1,0:T(8,128)}, u32[]{:S(2)}) copy-start(f32[96,192]{1,0:T(8,128)} %get-tuple-element.71) | copy-start | bytes 221188
  248.7 7.8 %copy-start.2 = (bf16[512,768]{1,0:T(8,128)(2,1)S(1)}, bf16[512,768]{1,0:T(8,128)(2,1)}, u32[]{:S(2)}) copy-start(bf16[512,768]{1,0:T(8,128)(2,1)} %get-tuple-element.155) | copy-start | bytes 2359300
  248.7 8.7 %copy-start.3 = (bf16[512,768]{1,0:T(8,128)(2,1)S(1)}, bf16[512,768]{1,0:T(8,128)(2,1)}, u32[]{:S(2)}) copy-start(bf16[512,768]{1,0:T(8,128)(2,1)} %get-tuple-element.156) | copy-start | bytes 2359300
  256.5 1.8 copy-start.5
  256.6 2.5 copy-start.4
where the time goes:
time: 260 us
  Pallas kernels  204 us (78%)
  local copies, waits for them, and re-layouts  26.1 us (10%)
  waiting for transfers between devices  19.2 us (7%)
  other arithmetic  5.11 us (2%)
  between operations  2.92 us (1%)
    pallas_call x1, Pallas kernels, attention_backward(): pl.pallas_call(functools.partial(backward_kernel, levels), out_shape=(jax...  78.9 us
    pallas_call x1, Pallas kernels, attention_forward(): pl.pallas_call(functools.partial(forward_kernel, levels), out_shape=(jax....  66 us
    pallas_call x1, Pallas kernels, feed_forward(): pl.pallas_call(feed_kernel, out_shape=(shape((D, hidden), bf), shape((D,...  30.5 us
    pallas_call x1, Pallas kernels, finish_layer(): pl.pallas_call(functools.partial(finish_kernel, levels), out_shape=(shape...  28.8 us
    ppermute x1, waiting for transfers between devices, local(): query_oth = lax.ppermute(query_col, 'seq', swap)  19.2 us
    unnamed x40, local copies, waits for them, and re-layouts  6.06 us
  transfers between devices with their start and end apart: 2, of which 1 were waited for; matrix products, arithmetic and copies ran while one was open for 2% of the time, Pallas kernels for 12%

commit v1 on v0

v1 whole, which is shorter than its diff:
```python
import functools
from types import SimpleNamespace
from typing import NamedTuple

import ml_dtypes
import numpy as np

import jax
import jax.numpy as jnp
from jax import lax
from jax.experimental import pallas as pl
from jax.experimental.pallas import tpu as pltpu
from jax.sharding import PartitionSpec as P

D = 768
DH = 64
NB = 512
SEG = 512
BOOKS = 4


EPS = 1e-05
TAU = 0.75
RIDGE = 1.0
SPREAD = 0.01
NEGATIVE = -1e30
MESH_ID = pl.DeviceIdType.MESH
VMEM_LIMIT = 60 * 2**20


def coefficient_tables(age_count, basis_n, seg_len):
    shrink = TAU ** np.arange(age_count, dtype=np.float64)
    inside = (np.arange(seg_len) + 0.5) / seg_len
    times = shrink[:, None] * (TAU + (1.0 - TAU) * inside[None, :])
    centres = (np.arange(basis_n) + 0.5) / basis_n
    offset = (times[:, None, :] - centres[None, :, None]) * basis_n
    basis = np.exp(-0.5 * offset * offset)
    gram = np.einsum("agx,ahx->gh", basis, basis) + RIDGE * np.eye(basis_n)
    table = np.linalg.solve(gram[None], basis)
    high = table.astype(ml_dtypes.bfloat16)
    lower = (table - high.astype(np.float64)).astype(ml_dtypes.bfloat16)
    return high, lower


LANES_OUT = 256


def head_of_lane(width):
    return lax.broadcasted_iota(jnp.int32, (1, width), 1) // DH


def head_masks(width):
    lane_head = head_of_lane(width)
    return [(lane_head == head).astype(jnp.float32).astype(jnp.bfloat16) for head in range(width // DH)]


def pick_heads(per_head, lane_head):
    chosen = per_head[0]
    for head in range(1, len(per_head)):
        chosen = jnp.where(lane_head == head, per_head[head], chosen)
    return chosen


def dot_rows(left, right):
    return lax.dot_general(left, right, (((1,), (1,)), ((), ())), preferred_element_type=jnp.float32)


def dot_plain(left, right):
    return lax.dot_general(left, right, (((1,), (0,)), ((), ())), preferred_element_type=jnp.float32)


def thirds(value):
    first = value.astype(jnp.bfloat16)
    rest = value - first.astype(jnp.float32)
    second = rest.astype(jnp.bfloat16)
    third = (rest - second.astype(jnp.float32)).astype(jnp.bfloat16)
    return first, second, third


def with_stats(block, stats):
    rows, width = block.shape
    spare = LANES_OUT - width
    lane = lax.broadcasted_iota(jnp.int32, (1, spare), 1)
    tail = jnp.zeros((rows, spare), jnp.float32)
    for index, column in enumerate(stats):
        for part, value in enumerate(thirds(column)):
            tail = jnp.where(lane == 3 * index + part, value.astype(jnp.float32), tail)
    return jnp.concatenate([block, tail.astype(jnp.bfloat16)], axis=1)


def stat_column(extended, width, index):
    lane = lax.broadcasted_iota(jnp.int32, (1, LANES_OUT), 1)
    start = width + 3 * index
    mine = (lane >= start) & (lane < start + 3)
    return jnp.sum(jnp.where(mine, extended.astype(jnp.float32), 0.0), axis=1, keepdims=True)


def stat_rows(extended, width, count):
    row = lax.broadcasted_iota(jnp.int32, (count, LANES_OUT), 0)
    lane = lax.broadcasted_iota(jnp.int32, (count, LANES_OUT), 1)
    start = width + 3 * row
    chooser = ((lane >= start) & (lane < start + 3)).astype(jnp.float32).astype(jnp.bfloat16)
    return dot_rows(chooser, extended)


def greet(levels, whole_tp=False):
    seq, tp = lax.axis_index("seq"), lax.axis_index("tp")
    level, side = seq // 2, seq % 2
    barrier = pltpu.get_barrier_semaphore()
    pl.semaphore_signal(barrier, inc=1, device_id=(2 * level + 1 - side, tp), device_id_type=MESH_ID)

    def one(step, unused):
        other = lax.rem(level + step, levels)
        pl.semaphore_signal(barrier, inc=1, device_id=(2 * other + side, tp), device_id_type=MESH_ID)
        return unused

    lax.fori_loop(1, levels, one, 0)
    if not whole_tp:
        return barrier, levels
    greet_tp()
    return barrier, levels + 2


class MemoryPlace(NamedTuple):
    loose: jax.Array
    centre: jax.Array
    spread: jax.Array
    height: jax.Array
    gap: jax.Array


def memory_place(query, spot_rows, in_head):
    width_sq = 1.0 / (NB * NB)
    centre = 1.0 / (
        1.0 + jnp.exp(-jnp.sum(jnp.where(in_head, query * spot_rows[0:1, :], 0.0), axis=1, keepdims=True))
    )
    loose = jnp.sum(jnp.where(in_head, query * spot_rows[1:2, :], 0.0), axis=1, keepdims=True)
    soft = jnp.maximum(loose, 0.0) + jnp.log(1.0 + jnp.exp(-jnp.abs(loose)))
    spread = SPREAD * soft + width_sq
    height = (1.0 / NB) * lax.rsqrt(spread)
    centres = (lax.broadcasted_iota(jnp.int32, (1, NB), 1).astype(jnp.float32) + 0.5) / NB
    return MemoryPlace(loose, centre, spread, height, centre - centres)


def forward_kernel(
    levels,
    tok_ref,
    norm_ref,
    weight_ref,
    bias_ref,
    doc_col_ref,
    doc_row_ref,
    key_mask_ref,
    past_ref,
    book_ref,
    spot_ref,
    table_ref,
    normed_ref,
    pair_ref,
    kv_out_ref,
    out_ref,
    lse_ref,
    heads_ref,
    coeff_ref,
    mem_ref,
    spot_row_ref,
    top_ref,
    total_ref,
    acc_ref,
    part_ref,
    part_in_ref,
    kv_send,
    kv_recv,
    pair_sem,
    part_sem,
    past_col_ref,
    past_oth_ref,
    table_in_ref,
    past_up,
    past_down,
    past_side,
    coeff_sems,
    table_sem,
):
    seq, tp = lax.axis_index("seq"), lax.axis_index("tp")
    level, side = seq // 2, seq % 2
    rows = tok_ref.shape[0]
    width = pair_ref.shape[2]
    heads = width // DH
    partner = (2 * level + 1 - side, tp)
    lane_head = head_of_lane(width)
    head_mask = head_masks(width)
    barrier, greetings = greet(levels, True)

    chunk = rows // 2
    past_col_ref[level] = past_ref[...]

    def past_copy(direction, from_level):
        block = past_col_ref.at[from_level]
        if direction == "side":
            sems, target, place = past_side, partner, past_oth_ref.at[from_level]
        elif direction == "up":
            sems, target, place = past_up, (lax.rem(2 * level + 2, 2 * levels) + side, tp), block
        else:
            sems, target, place = past_down, (lax.rem(2 * (level + levels - 1), 2 * levels) + side, tp), block
        return pltpu.make_async_remote_copy(
            block,
            place,
            sems.at[0, from_level],
            sems.at[1, from_level],
            device_id=target,
            device_id_type=MESH_ID,
        )

    pl.semaphore_wait(barrier, greetings)

    def pass_past(from_level, up, down):
        past_copy("side", from_level).start()
        if up:

            @pl.when(level < levels - 1)
            def _():
                past_copy("up", from_level).start()

        if down:

            @pl.when(level > 0)
            def _():
                past_copy("down", from_level).start()

    pass_past(level, True, True)

    def project(index, unused):
        here = pl.ds(pl.multiple_of(index * chunk, chunk), chunk)
        x = tok_ref[here, :].astype(jnp.float32)
        centred = x - jnp.mean(x, axis=1, keepdims=True)
        variance = jnp.mean(centred * centred, axis=1, keepdims=True)
        a = centred * lax.rsqrt(variance + EPS) * norm_ref[0:1, :] + norm_ref[1:2, :]
        a = a.astype(jnp.bfloat16)
        normed_ref[here, :] = a
        mixed = (dot_plain(a, weight_ref[...]) + bias_ref[0:1, :]).astype(jnp.bfloat16)
        query = mixed[:, :width] * jnp.bfloat16(DH**-0.5)
        pair_ref[0, here, :] = query
        kv_out_ref[level, here, :] = mixed[:, width:]
        return unused

    lax.fori_loop(0, rows // chunk, project, 0)
    kv_out_ref[level, rows:, :] = key_mask_ref[...]

    pair_copy = pltpu.make_async_remote_copy(
        pair_ref.at[0], pair_ref.at[1], pair_sem.at[0], pair_sem.at[1], device_id=partner, device_id_type=MESH_ID
    )
    pair_copy.start()

    def kv_copy(from_level):
        return pltpu.make_async_remote_copy(
            kv_out_ref.at[from_level],
            kv_out_ref.at[from_level],
            kv_send.at[from_level],
            kv_recv.at[from_level],
            device_id=(lax.rem(2 * level + 2, 2 * levels) + side, tp),
            device_id_type=MESH_ID,
        )

    @pl.when(level < levels - 1)
    def _():
        kv_copy(level).start()

    top_ref[...] = jnp.full(top_ref.shape, NEGATIVE, jnp.float32)
    total_ref[...] = jnp.zeros(total_ref.shape, jnp.float32)
    acc_ref[...] = jnp.zeros(acc_ref.shape, jnp.float32)

    doc_first = doc_row_ref[0:1, 0:1]
    def reach_of(here):
        docs = doc_col_ref[here, :]
        last = (level == levels - 1) & (side == 1)
        return jnp.where(last & (docs != doc_first), NEGATIVE, 0.0)

    def fold(slot, from_level, mask_kind):
        mask_rows = kv_out_ref[from_level, rows:, :].astype(jnp.float32)
        key_mask = jnp.concatenate([mask_rows[0:1, : rows // 2], mask_rows[1:2, : rows // 2]], axis=1)

        def part(index, unused):
            here = pl.ds(pl.multiple_of(index * chunk, chunk), chunk)
            query = pair_ref[slot, here, :]
            keys = kv_out_ref[from_level, :rows, :width]
            vals = kv_out_ref[from_level, :rows, width:]
            if mask_kind == "own":
                q_pos = index * chunk + lax.broadcasted_iota(jnp.int32, (chunk, rows), 0)
                k_pos = lax.broadcasted_iota(jnp.int32, (chunk, rows), 1)
                visible = (q_pos >= k_pos) & (doc_col_ref[here, :] == doc_row_ref[0:1, :])
            products, scales = [], []
            for head in range(heads):
                scores = dot_rows(query * head_mask[head], keys)
                old_top = top_ref[slot, head, here, :]
                if mask_kind == "own":
                    scores = jnp.where(visible, scores, NEGATIVE)
                    reach = 0.0
                else:
                    scores = scores + key_mask
                    reach = jnp.where(slot == 0, reach_of(here), 0.0)
                new_top = jnp.maximum(old_top, jnp.max(scores, axis=1, keepdims=True) + reach)
                weights = jnp.exp(scores - (new_top - reach))
                scale = jnp.exp(old_top - new_top)
                top_ref[slot, head, here, :] = new_top
                total_ref[slot, head, here, :] = total_ref[slot, head, here, :] * scale + jnp.sum(
                    weights, axis=1, keepdims=True
                )
                products.append(dot_plain(weights.astype(jnp.bfloat16), vals))
                scales.append(scale)
            acc_ref[slot, here, :] = acc_ref[slot, here, :] * pick_heads(scales, lane_head) + pick_heads(
                products, lane_head
            )
            return unused

        lax.fori_loop(0, rows // chunk, part, 0)

    fold(0, level, "own")
    pair_copy.wait()

    @pl.when(side == 0)
    def _():
        fold(1, level, "off")

    def keys_arrived(step):
        from_level = level - step
        kv_copy(from_level).wait_recv()

        @pl.when(level < levels - 1)
        def _():
            kv_copy(from_level).start()

        def both(slot, inner):
            fold(slot, from_level, "off")
            return inner

        lax.fori_loop(0, 2, both, 0)

    def arrived(step, unused):
        @pl.when(level >= step)
        def _():
            past_copy("up", level - step).wait_recv()
            pass_past(level - step, True, False)

        @pl.when(level + step < levels)
        def _():
            past_copy("down", level + step).wait_recv()
            pass_past(level + step, False, True)

        @pl.when((level >= step) & (step < levels - 1))
        def _():
            keys_arrived(step)

        return unused

    lax.fori_loop(1, levels, arrived, 0)

    def from_side(other, unused):
        past_copy("side", other).wait_recv()
        return unused

    lax.fori_loop(0, levels, from_side, 0)
    own_book = book_ref[0:1, :]
    time_half = rows // 2
    ages = table_ref.shape[0]

    def one_age(age, total):
        table_copy = pltpu.make_async_copy(table_ref.at[age], table_in_ref, table_sem)
        table_copy.start()

        def one_level(other, found):
            for blocks_ref in (past_col_ref, past_oth_ref):
                mark = blocks_ref[other, time_half:, :].astype(jnp.float32)
                chosen = (mark[0:1, :] == own_book) & (mark[1:2, :] == age.astype(jnp.float32))
                found = jnp.where(chosen, blocks_ref[other, :time_half, :].astype(jnp.float32), found)
            return found

        found = lax.fori_loop(
            0, levels, one_level, jnp.zeros((time_half, 2 * width), jnp.float32)
        ).astype(jnp.bfloat16)
        table_copy.wait()
        for index in range(2):
            table = table_in_ref[index]
            total = total + (
                dot_plain(table[:, :time_half], found)[:, :width]
                + dot_plain(table[:, time_half:], found)[:, width:]
            )
        return total

    coeff = lax.fori_loop(0, ages, one_age, jnp.zeros((NB, width), jnp.float32))
    coeff_ref[tp] = coeff.astype(jnp.bfloat16)

    def coeff_copy(kind, slot, index):
        return swap_with(kind, coeff_ref.at[slot], coeff_ref.at[slot], (coeff_sems.at[0], coeff_sems.at[1]), index)

    core_mate, chip_mate = tp + 1 - 2 * (tp % 2), lax.rem(tp + 2, 4)
    coeff_copy("chip", tp, 0).start()
    coeff_copy("core", tp, 1).start()

    @pl.when(level == levels - 1)
    def _():
        keys_arrived(levels - 1)

    def finish(index, unused):
        here = pl.ds(pl.multiple_of(index * chunk, chunk), chunk)
        totals = [total_ref[1, head, here, :] for head in range(heads)]
        tops = [top_ref[1, head, here, :] for head in range(heads)]
        some = [value > 0.0 for value in totals]
        inverse = [jnp.where(ok, 1.0 / jnp.where(ok, value, 1.0), 0.0) for ok, value in zip(some, totals)]
        logs = [
            jnp.where(ok, top + jnp.log(jnp.where(ok, value, 1.0)), NEGATIVE)
            for ok, top, value in zip(some, tops, totals)
        ]
        share = (acc_ref[1, here, :] * pick_heads(inverse, lane_head)).astype(jnp.bfloat16)
        part_ref[here, :] = with_stats(share, logs)
        return unused

    lax.fori_loop(0, rows // chunk, finish, 0)
    part_copy = pltpu.make_async_remote_copy(
        part_ref, part_in_ref, part_sem.at[0], part_sem.at[1], device_id=partner, device_id_type=MESH_ID
    )
    part_copy.start()

    coeff_copy("chip", chip_mate, 0).wait_recv()
    coeff_copy("core", chip_mate, 2).start()
    coeff_copy("core", core_mate, 1).wait_recv()
    coeff_copy("core", lax.rem(core_mate + 2, 4), 2).wait_recv()
    memory = jnp.zeros((NB, 2 * width), jnp.float32)
    for slot in range(4):
        memory = memory + dot_plain(
            coeff_ref[slot], weight_ref[slot * width : (slot + 1) * width, width:]
        )
    mem_ref[...] = memory.astype(jnp.bfloat16)
    for index in range(2):
        spots = spot_ref[8 * index : 8 * index + 8, :]
        row = sum(dot_plain(third, mem_ref[:, :width]) for third in thirds(spots))
        spot_row_ref[index : index + 1, :] = pick_heads(
            [row[head : head + 1, :] for head in range(heads)], lane_head
        )
    part_copy.wait()

    def merge(index, unused):
        here = pl.ds(pl.multiple_of(index * chunk, chunk), chunk)
        reach = reach_of(here)
        received = part_in_ref[here, :]
        mine, theirs, columns = [], [], []
        for head in range(heads):
            total = total_ref[0, head, here, :]
            own_log = top_ref[0, head, here, :] + jnp.log(total)
            other_log = stat_column(received, width, head) + reach
            high = jnp.maximum(own_log, other_log)
            both_log = high + jnp.log(jnp.exp(own_log - high) + jnp.exp(other_log - high))
            mine.append(jnp.exp(own_log - both_log) / total)
            theirs.append(jnp.exp(other_log - both_log))
            columns.append(both_log)
        attended = acc_ref[0, here, :] * pick_heads(mine, lane_head) + received[:, :width].astype(
            jnp.float32
        ) * pick_heads(theirs, lane_head)
        out_ref[here, :] = attended
        query = pair_ref[0, here, :].astype(jnp.float32)
        reads = []
        for head in range(heads):
            place = memory_place(query, spot_row_ref[0:2, :], lane_head == head)
            density = place.height * jnp.exp(place.gap * place.gap * (-0.5 / place.spread))
            reads.append(dot_plain(density.astype(jnp.bfloat16), mem_ref[:, width:]))
        heads_ref[here, :] = (attended + pick_heads(reads, lane_head)).astype(jnp.bfloat16)
        lane = lax.broadcasted_iota(jnp.int32, (1, 8), 1)
        packed = jnp.zeros((chunk, 8), jnp.float32)
        for head in range(heads):
            packed = jnp.where(lane == head, columns[head], packed)
        lse_ref[here, :] = packed
        return unused

    lax.fori_loop(0, rows // chunk, merge, 0)

    coeff_copy("chip", tp, 0).wait_send()
    coeff_copy("core", tp, 1).wait_send()
    coeff_copy("core", chip_mate, 2).wait_send()

    def past_sent(other, unused):
        past_copy("side", other).wait_send()

        @pl.when((level < levels - 1) & (other <= level))
        def _():
            past_copy("up", other).wait_send()

        @pl.when((level > 0) & (other >= level))
        def _():
            past_copy("down", other).wait_send()

        return unused

    lax.fori_loop(0, levels, past_sent, 0)

    @pl.when(level < levels - 1)
    def _():
        def sent_up(from_level, unused):
            kv_copy(from_level).wait_send()
            return unused

        lax.fori_loop(0, level + 1, sent_up, 0)


def attention_forward(levels, tokens, norm, weight, bias, doc_ids, key_mask, past, book, spots, table):
    rows = tokens.shape[0]
    width = weight.shape[1] // 3
    heads = width // DH
    vmem = pl.BlockSpec(memory_space=pltpu.VMEM)
    dma = pltpu.SemaphoreType.DMA
    return pl.pallas_call(
        functools.partial(forward_kernel, levels),
        out_shape=(
            jax.ShapeDtypeStruct((rows, D), jnp.bfloat16),
            jax.ShapeDtypeStruct((2, rows, width), jnp.bfloat16),
            jax.ShapeDtypeStruct((levels, rows + 16, 2 * width), jnp.bfloat16),
            jax.ShapeDtypeStruct((rows, width), jnp.float32),
            jax.ShapeDtypeStruct((rows, 8), jnp.float32),
            jax.ShapeDtypeStruct((rows, width), jnp.bfloat16),
            jax.ShapeDtypeStruct((4, NB, width), jnp.bfloat16),
            jax.ShapeDtypeStruct((NB, 2 * width), jnp.bfloat16),
            jax.ShapeDtypeStruct((8, width), jnp.float32),
        ),
        in_specs=[vmem] * 10 + [pl.BlockSpec(memory_space=pl.ANY)],
        out_specs=(vmem,) * 9,
        scratch_shapes=[
            pltpu.VMEM((2, heads, rows, 1), jnp.float32),
            pltpu.VMEM((2, heads, rows, 1), jnp.float32),
            pltpu.VMEM((2, rows, width), jnp.float32),
            pltpu.VMEM((rows, LANES_OUT), jnp.bfloat16),
            pltpu.VMEM((rows, LANES_OUT), jnp.bfloat16),
            dma((levels,)),
            dma((levels,)),
            dma((2,)),
            dma((2,)),
            pltpu.VMEM((levels,) + past.shape, jnp.bfloat16),
            pltpu.VMEM((levels,) + past.shape, jnp.bfloat16),
            pltpu.VMEM(table.shape[1:], jnp.bfloat16),
            dma((2, levels)),
            dma((2, levels)),
            dma((2, levels)),
            dma((2, 3)),
            dma(()),
        ],
        name="attention_forward",
        compiler_params=pltpu.CompilerParams(
            collective_id=1, has_side_effects=True, vmem_limit_bytes=VMEM_LIMIT
        ),
    )(
        tokens,
        norm,
        weight,
        bias,
        doc_ids[:, None],
        doc_ids[None, :],
        key_mask,
        past,
        book,
        spots,
        table,
    )


def column_copy(block_ref, from_level, landing_ref, send_sem, recv_sem, to_level):
    seq, tp = lax.axis_index("seq"), lax.axis_index("tp")
    return pltpu.make_async_remote_copy(
        block_ref,
        landing_ref.at[from_level],
        send_sem.at[to_level],
        recv_sem.at[from_level],
        device_id=(2 * to_level + seq % 2, tp),
        device_id_type=MESH_ID,
    )


class Scatter:
    def __init__(self, levels, blocks, plane_in, plane_sum, column_in, sems):
        self.levels, self.blocks = levels, blocks
        self.plane_in, self.plane_sum, self.column_in = plane_in, plane_sum, column_in
        self.plane_send, self.plane_recv, self.column_send, self.column_recv = sems
        seq, tp = lax.axis_index("seq"), lax.axis_index("tp")
        self.level, self.side, self.tp = seq // 2, seq % 2, tp

    def plane_copy(self, to_level):
        return pltpu.make_async_remote_copy(
            self.blocks.at[2 * to_level + 1 - self.side],
            self.plane_in.at[to_level],
            self.plane_send.at[to_level],
            self.plane_recv.at[to_level],
            device_id=(2 * self.level + 1 - self.side, self.tp),
            device_id_type=MESH_ID,
        )

    def swap_copy(self, from_level, to_level):
        return column_copy(
            self.plane_sum.at[to_level], from_level, self.column_in, self.column_send, self.column_recv, to_level
        )

    def loop(self, first, body):
        def one(step, unused):
            body(lax.rem(self.level + step, self.levels))
            return unused

        lax.fori_loop(first, self.levels, one, 0)

    def start(self):
        self.loop(0, lambda other: self.plane_copy(other).start())

    def middle(self):
        def one(other):
            self.plane_copy(other).wait_recv()
            total = self.blocks[2 * other + self.side].astype(jnp.float32) + self.plane_in[other].astype(
                jnp.float32
            )
            self.plane_sum[other] = total.astype(jnp.bfloat16)
            self.swap_copy(self.level, other).start()

        self.loop(1, one)

    def finish(self, out_ref):
        self.plane_copy(self.level).wait_recv()
        out_ref[...] = self.blocks[2 * self.level + self.side].astype(jnp.float32) + self.plane_in[
            self.level
        ].astype(jnp.float32)

        def one(other):
            self.swap_copy(other, self.level).wait_recv()
            out_ref[...] += self.column_in[other].astype(jnp.float32)

        self.loop(1, one)
        self.loop(0, lambda other: self.plane_copy(other).wait_send())
        self.loop(1, lambda other: self.swap_copy(self.level, other).wait_send())

    @staticmethod
    def scratch(levels, rows, width):
        buffer = pltpu.VMEM((levels, rows, width), jnp.bfloat16)
        return [buffer] * 3 + [pltpu.SemaphoreType.DMA((levels,))] * 4


class SmallSum:
    def __init__(self, levels, small, plane_in, column_in, sems):
        self.levels, self.small, self.plane_in, self.column_in = levels, small, plane_in, column_in
        self.plane_sem, self.column_send, self.column_recv = sems
        seq, tp = lax.axis_index("seq"), lax.axis_index("tp")
        self.level, self.side, self.tp = seq // 2, seq % 2, tp

    def plane_copy(self):
        return pltpu.make_async_remote_copy(
            self.small,
            self.plane_in,
            self.plane_sem.at[0],
            self.plane_sem.at[1],
            device_id=(2 * self.level + 1 - self.side, self.tp),
            device_id_type=MESH_ID,
        )

    def swap_copy(self, from_level, to_level):
        return column_copy(
            self.column_in.at[from_level], from_level, self.column_in, self.column_send, self.column_recv, to_level
        )

    def loop(self, body):
        def one(step, unused):
            body(lax.rem(self.level + step, self.levels))
            return unused

        lax.fori_loop(1, self.levels, one, 0)

    def start(self):
        self.plane_copy().start()

    def middle(self):
        self.plane_copy().wait()
        self.column_in[self.level] = self.small[...] + self.plane_in[...]
        self.loop(lambda other: self.swap_copy(self.level, other).start())

    def finish(self, out_ref):
        self.loop(lambda other: self.swap_copy(other, self.level).wait_recv())
        self.loop(lambda other: self.swap_copy(self.level, other).wait_send())
        out_ref[...] = self.column_in[0]

        def one(other, unused):
            out_ref[...] += self.column_in[other]
            return unused

        lax.fori_loop(1, self.levels, one, 0)

    @staticmethod
    def scratch(levels, shape):
        dma = pltpu.SemaphoreType.DMA
        return [
            pltpu.VMEM(shape, jnp.float32),
            pltpu.VMEM((levels,) + shape, jnp.float32),
            dma((2,)),
            dma((levels,)),
            dma((levels,)),
        ]


def tp_partner(kind):
    seq, tp = lax.axis_index("seq"), lax.axis_index("tp")
    if kind == "core":
        return (seq, tp + 1 - 2 * (tp % 2))
    return (seq, lax.rem(tp + 2, 4))


def greet_tp():
    barrier = pltpu.get_barrier_semaphore()
    for kind in ("core", "chip"):
        pl.semaphore_signal(barrier, inc=1, device_id=tp_partner(kind), device_id_type=MESH_ID)
    return barrier, 2


def swap_with(kind, source, target, sems, index):
    send, recv = sems
    return pltpu.make_async_remote_copy(
        source, target, send.at[index], recv.at[index], device_id=tp_partner(kind), device_id_type=MESH_ID
    )


class TpSum:
    def __init__(self, core_out, core_in, chip_out, chip_in, sems):
        self.core_out, self.core_in, self.chip_out, self.chip_in = core_out, core_in, chip_out, chip_in
        self.core_sems, self.chip_sems = sems[:2], sems[2:]

    def core_copy(self, part):
        return swap_with("core", self.core_out.at[part], self.core_in.at[part], self.core_sems, part)

    def chip_copy(self, part):
        return swap_with("chip", self.chip_out.at[part], self.chip_in.at[part], self.chip_sems, part)

    def start(self, part, for_other_core):
        self.core_out[part] = for_other_core.astype(jnp.bfloat16)
        self.core_copy(part).start()

    def middle(self, part, own):
        self.core_copy(part).wait()
        self.chip_out[part] = (own + self.core_in[part].astype(jnp.float32)).astype(jnp.bfloat16)
        self.chip_copy(part).start()

    def result(self, part):
        self.chip_copy(part).wait()
        return self.chip_out[part].astype(jnp.float32) + self.chip_in[part].astype(jnp.float32)

    @staticmethod
    def scratch(parts, rows, width):
        buffer = pltpu.VMEM((parts, rows, width), jnp.bfloat16)
        return [buffer] * 4 + [pltpu.SemaphoreType.DMA((parts,))] * 4

    COUNT = 8


class RowShare:
    def __init__(self, whole, rows, sems):
        self.whole, self.rows, self.sems = whole, rows, sems

    def copy(self, part, start):
        here = self.whole.at[pl.ds(pl.multiple_of(start, self.rows), self.rows), :]
        return swap_with("core", here, here, self.sems, part)


def normalize(v):
    centred = v - jnp.mean(v, axis=1, keepdims=True)
    scale = lax.rsqrt(jnp.mean(centred * centred, axis=1, keepdims=True) + EPS)
    return centred * scale, scale


def norm_back(grad, nhat, scale, gain):
    inner = grad * gain
    return (
        inner
        - jnp.mean(inner, axis=1, keepdims=True)
        - nhat * jnp.mean(inner * nhat, axis=1, keepdims=True)
    ) * scale


def gelu_and_slope(f):
    root = (2.0 / np.pi) ** 0.5
    square = f * f
    bend = jnp.tanh(root * f * (1.0 + 0.044715 * square))
    half = 0.5 * (1.0 + bend)
    slope = half + 0.5 * f * (1.0 - bend * bend) * (root * (1.0 + 3.0 * 0.044715 * square))
    return f * half, slope


def dot_columns(left, right):
    return lax.dot_general(left, right, (((0,), (0,)), ((), ())), preferred_element_type=jnp.float32)


def column_sum(v):
    return jnp.sum(v, axis=0, keepdims=True)


class LateOutput:
    def __init__(self, base, own, other, whole, sems):
        self.base, self.own, self.other, self.whole = base, own, other, whole
        self.half = own.shape[0]
        self.core_in, self.chip_out, self.chip_in = sems[:3]
        self.core_sems, self.chip_sems, self.share_sems = sems[3:5], sems[5:7], sems[7:9]
        self.share = RowShare(whole, self.half, self.share_sems)
        self.core = lax.axis_index("tp") % 2

    COUNT = 9

    def core_copy(self):
        return swap_with("core", self.other, self.core_in, self.core_sems, 0)

    def chip_copy(self):
        return swap_with("chip", self.chip_out, self.chip_in, self.chip_sems, 0)

    def start(self):
        self.core_copy().start()

    def middle(self):
        self.core_copy().wait()
        self.chip_out[...] = (self.own[...] + self.core_in[...].astype(jnp.float32)).astype(jnp.bfloat16)
        self.chip_copy().start()

    def late(self):
        self.chip_copy().wait()
        total = self.chip_out[...].astype(jnp.float32) + self.chip_in[...].astype(jnp.float32)
        here = pl.ds(pl.multiple_of(self.core * self.half, self.half), self.half)
        self.whole[here, :] = (self.base[...] + total).astype(jnp.bfloat16)
        self.share.copy(0, self.core * self.half).start()

    def finish(self):
        self.share.copy(0, (1 - self.core) * self.half).wait_recv()
        self.share.copy(0, self.core * self.half).wait_send()

    @staticmethod
    def scratch(half, width):
        buffer = pltpu.VMEM((half, width), jnp.bfloat16)
        return [buffer] * 3 + [pltpu.SemaphoreType.DMA((1,))] * 6


PARTS = 2


def back_kernel(levels, names, *refs):
    r = SimpleNamespace(**dict(zip(names, refs)))
    seq, tp = lax.axis_index("seq"), lax.axis_index("tp")
    level, side, core = seq // 2, seq % 2, tp % 2
    rows, width = r.heads.shape
    heads = width // DH
    half = rows // 2
    size = half // PARTS
    partner = (2 * level + 1 - side, tp)
    lane_head = head_of_lane(width)
    head_mask = head_masks(width)
    chunk = rows // 2
    staged = hasattr(r, "stage_query")

    first, second, third = (
        TpSum(*(getattr(r, f"{name}_{i}") for i in range(4)), [getattr(r, f"{name}_{i}") for i in range(4, 8)])
        for name in ("first", "second", "third")
    )
    scatters = [
        Scatter(
            levels,
            getattr(r, f"{name}_blocks"),
            *(getattr(r, f"{name}_{i}") for i in range(3)),
            [getattr(r, f"{name}_{i}") for i in range(3, 7)],
        )
        for name in ("proj", "fc", "out", "qkv")
    ]
    small = SmallSum(levels, r.small, r.small_0, r.small_1, (r.small_2, r.small_3, r.small_4))
    late = LateOutput(
        r.base, r.own_two, r.other_two, r.output, [getattr(r, f"late_{i}") for i in range(LateOutput.COUNT)]
    )
    c_share = RowShare(r.c, size, (r.share_0, r.share_1))
    e_share = RowShare(r.e1, size, (r.share_2, r.share_3))
    token_share = RowShare(r.tokens_out, size, (r.share_4, r.share_5))
    gain, offset, out_b, fc_b, proj_b, first_gain = (r.vec[i : i + 1, :] for i in range(6))
    barrier, greetings = greet(levels, True)

    def span(start, count=size):
        return pl.ds(pl.multiple_of(start, size), count)

    def mine(part):
        return core * half + part * size

    def theirs(part):
        return (1 - core) * half + part * size

    def block_of(blocks_ref, from_level, place):
        if not staged:
            return blocks_ref.at[from_level]
        target = getattr(r, "stage_" + place)
        copy = pltpu.make_async_copy(blocks_ref.at[from_level], target, r.stage_sem)
        copy.start()
        copy.wait()
        return target

    def down_copy(source_ref, landing_ref, sems, from_level, to_level):
        send, recv = sems
        return pltpu.make_async_remote_copy(
            source_ref,
            landing_ref.at[from_level],
            send.at[to_level],
            recv.at[from_level],
            device_id=(2 * to_level + side, tp),
            device_id_type=MESH_ID,
        )

    def side_copy(source_ref, landing_ref, sems, from_level):
        send, recv = sems
        return pltpu.make_async_remote_copy(
            source_ref,
            landing_ref.at[from_level],
            send.at[from_level],
            recv.at[from_level],
            device_id=partner,
            device_id_type=MESH_ID,
        )

    def query_down(from_level, to_level):
        return down_copy(r.pair.at[0], r.query_col, (r.qd_send, r.qd_recv), from_level, to_level)

    def query_side(from_level):
        return side_copy(r.query_col.at[from_level], r.query_oth, (r.qs_send, r.qs_recv), from_level)

    def grad_down(from_level, to_level):
        return down_copy(r.far, r.grad_col, (r.gd_send, r.gd_recv), from_level, to_level)

    def grad_side(from_level):
        return side_copy(r.grad_col.at[from_level], r.grad_oth, (r.gs_send, r.gs_recv), from_level)

    def own_grad_side():
        return side_copy(r.far, r.grad_oth, (r.gs_send, r.gs_recv), level)

    def each_below(body):
        def one(step, unused):
            body(level - step)
            return unused

        lax.fori_loop(1, level + 1, one, 0)

    def each_above(body):
        def one(step, unused):
            body(level + step)
            return unused

        lax.fori_loop(1, levels - level, one, 0)

    pl.semaphore_wait(barrier, greetings)
    each_below(lambda other: query_down(level, other).start())

    for part in range(PARTS):
        first.start(part, dot_plain(r.heads[span(theirs(part)), :], r.out_w[...]))
        r.own[span(part * size), :] = dot_plain(r.heads[span(mine(part)), :], r.out_w[...])
    for part in range(PARTS):
        first.middle(part, r.own[span(part * size), :])

    def early(index, unused):
        here = span(index * size)
        r.pull[here, :] = dot_rows(r.cot[here, :], r.proj_w[...])
        return unused

    lax.fori_loop(0, rows // size, early, 0)
    r.small[...] = jnp.zeros(r.small.shape, jnp.float32)
    r.fold[...] = jnp.zeros(r.fold.shape, jnp.float32)
    r.small[6:7, :] = column_sum(r.cot[...].astype(jnp.float32))

    def feed(start):
        here = span(start)
        f = dot_plain(r.c[here, :], r.fc_w[...]) + fc_b
        u, slope = gelu_and_slope(f)
        r.u[here, :] = u.astype(jnp.bfloat16)
        ef = (r.pull[here, :] * slope).astype(jnp.bfloat16)
        r.ef[here, :] = ef
        return dot_rows(ef, r.fc_w[...])

    for part in range(PARTS):
        total = first.result(part) + out_b
        h1 = r.tok[span(mine(part)), :].astype(jnp.float32) + total
        r.h1[span(part * size), :] = h1
        nhat, scale = normalize(h1)
        r.c[span(mine(part)), :] = (nhat * gain + offset).astype(jnp.bfloat16)
        c_share.copy(part, mine(part)).start()
        r.own[span(part * size), :] = feed(mine(part))
        c_share.copy(part, theirs(part)).wait_recv()
        second.start(part, feed(theirs(part)))
        r.other_two[span(part * size), :] = dot_plain(r.u[span(theirs(part)), :], r.proj_w[...]).astype(
            jnp.bfloat16
        )
        r.own_two[span(part * size), :] = dot_plain(r.u[span(mine(part)), :], r.proj_w[...])
        second.middle(part, r.own[span(part * size), :])

    r.base[...] = r.h1[...] + proj_b
    bite = 384

    def weight_blocks(blocks_ref, left_ref, right, extra=None):
        slab = blocks_ref.shape[1]
        for index in range(D // bite):
            value = dot_columns(left_ref[:, index * bite : (index + 1) * bite], right)
            if extra is not None:
                value = value + extra[index * bite : (index + 1) * bite, :]
            for place in range(bite // slab):
                blocks_ref[index * (bite // slab) + place] = value[
                    place * slab : (place + 1) * slab
                ].astype(jnp.bfloat16)

    weight_blocks(r.proj_blocks, r.cot, r.u[...])
    scatters[0].start()
    weight_blocks(r.fc_blocks, r.c, r.ef[...])
    scatters[1].start()

    def query_on(other):
        query_down(other, level).wait_recv()
        query_side(other).start()

    each_above(query_on)

    gain_sum = jnp.zeros((1, D), jnp.float32)
    offset_sum = jnp.zeros((1, D), jnp.float32)
    out_sum = jnp.zeros((1, D), jnp.float32)
    for part in range(PARTS):
        grad = second.result(part)
        nhat, scale = normalize(r.h1[span(part * size), :])
        gain_sum = gain_sum + column_sum(grad * nhat)
        offset_sum = offset_sum + column_sum(grad)
        mid = r.cot[span(mine(part)), :].astype(jnp.float32) + norm_back(grad, nhat, scale, gain)
        r.mid[span(part * size), :] = mid
        e1 = mid.astype(jnp.bfloat16)
        out_sum = out_sum + column_sum(e1.astype(jnp.float32))
        r.e1[span(mine(part)), :] = e1
        e_share.copy(part, mine(part)).start()
        r.grad[span(mine(part)), :] = dot_rows(e1, r.out_w[...]).astype(jnp.bfloat16)
    r.fold[2:3, :] = gain_sum
    r.fold[3:4, :] = offset_sum
    r.fold[4:5, :] = out_sum
    for part in range(PARTS):
        e_share.copy(part, theirs(part)).wait_recv()
        r.grad[span(theirs(part)), :] = dot_rows(r.e1[span(theirs(part)), :], r.out_w[...]).astype(jnp.bfloat16)

    doc_first = r.doc_row[0:1, 0:1]
    last = (level == levels - 1) & (side == 1)

    def prepare(index, unused):
        here = pl.ds(pl.multiple_of(index * chunk, chunk), chunk)
        grad = r.grad[here, :]
        product = grad.astype(jnp.float32) * r.attended[here, :]
        far = jnp.where(last & (r.doc_col[here, :] != doc_first), -NEGATIVE, 0.0)
        lses = [r.lse[here, head : head + 1] for head in range(heads)]
        deltas = [
            jnp.sum(jnp.where(lane_head == head, product, 0.0), axis=1, keepdims=True)
            for head in range(heads)
        ]
        r.near[here, :] = with_stats(grad, lses + deltas)
        r.far[here, :] = with_stats(grad, [lse + far for lse in lses] + deltas)
        for head in range(heads):
            r.near_lse[head, here, :] = lses[head]
            r.stat[0, head, here, :] = lses[head] + far
            r.stat[0, heads + head, here, :] = deltas[head]
        return unused

    lax.fori_loop(0, rows // chunk, prepare, 0)
    own_grad_side().start()
    each_below(lambda other: grad_down(level, other).start())
    late.start()
    weight_blocks(r.out_blocks, r.e1, r.heads[...])
    scatters[2].start()
    r.small[5:6, :] = column_sum(r.ef[...].astype(jnp.float32))

    r.mem_acc[...] = jnp.zeros(r.mem_acc.shape, jnp.float32)
    r.pulls[...] = jnp.zeros(r.pulls.shape, jnp.float32)

    def memory_back(index, unused):
        here = pl.ds(pl.multiple_of(index * chunk, chunk), chunk)
        query = r.pair[0, here, :].astype(jnp.float32)
        grad = r.grad[here, :]
        val_parts, mu_pulls, sigma_pulls = [], [], []
        for head in range(heads):
            place = memory_place(query, r.spot_rows[0:2, :], lane_head == head)
            slope = place.gap / place.spread
            square = place.gap * slope
            density = place.height * jnp.exp(-0.5 * square)
            val_parts.append(dot_columns(density.astype(jnp.bfloat16), grad))
            weighed = dot_rows(grad * head_mask[head], r.mem[:, width:]) * density
            to_centre = -jnp.sum(weighed * slope, axis=1, keepdims=True)
            to_spread = 0.5 * jnp.sum(weighed * (square - 1.0), axis=1, keepdims=True) / place.spread
            mu_pulls.append(to_centre * place.centre * (1.0 - place.centre))
            sigma_pulls.append(to_spread * SPREAD / (1.0 + jnp.exp(-place.loose)))
        mu_pull, sigma_pull = pick_heads(mu_pulls, lane_head), pick_heads(sigma_pulls, lane_head)
        r.dq[0, here, :] = mu_pull * r.spot_rows[0:1, :] + sigma_pull * r.spot_rows[1:2, :]
        r.mem_acc[...] += pick_heads(val_parts, lane_head)
        r.pulls[0:1, :] += column_sum(mu_pull * query)
        r.pulls[1:2, :] += column_sum(sigma_pull * query)
        return unused

    lax.fori_loop(0, rows // chunk, memory_back, 0)
    by_head = lax.broadcasted_iota(jnp.int32, (8, 1), 0) == lane_head
    pulls = [jnp.where(by_head, r.pulls[i : i + 1, :], 0.0) for i in range(2)]
    for index in range(2):
        spot_grad = sum(dot_rows(part, r.mem[:, :width]) for part in thirds(pulls[index]))
        r.small[8 + heads * index : 8 + heads * (index + 1), :NB] = spot_grad[:heads, :]
    key_grad = dot_columns(
        r.spots[...].astype(jnp.bfloat16), jnp.concatenate(pulls, axis=0).astype(jnp.bfloat16)
    )
    r.mem_grad[...] = jnp.concatenate([key_grad, r.mem_acc[...]], axis=1).astype(jnp.bfloat16)
    scatters[0].middle()

    r.dq[1] = jnp.zeros((rows, width), jnp.float32)
    r.dk[...] = jnp.zeros(r.dk.shape, jnp.float32)
    r.dv[...] = jnp.zeros(r.dv.shape, jnp.float32)

    def query_fold(slot, grad_ref, block_ref, own):
        if not own:
            mask_rows = block_ref[rows:, :].astype(jnp.float32)
            key_mask = jnp.concatenate([mask_rows[0:1, :half], mask_rows[1:2, :half]], axis=1)

        def part(index, unused):
            here = pl.ds(pl.multiple_of(index * chunk, chunk), chunk)
            query = r.pair[slot, here, :]
            grad = grad_ref[here, :width]
            keys = block_ref[:rows, :width]
            vals = block_ref[:rows, width:]
            if own:
                q_pos = index * chunk + lax.broadcasted_iota(jnp.int32, (chunk, rows), 0)
                k_pos = lax.broadcasted_iota(jnp.int32, (chunk, rows), 1)
                visible = (q_pos >= k_pos) & (r.doc_col[here, :] == r.doc_row[0:1, :])
            products = []
            for head in range(heads):
                scores = dot_rows(query * head_mask[head], keys)
                if own:
                    scores = jnp.where(visible, scores, NEGATIVE)
                    lse = r.near_lse[head, here, :]
                else:
                    scores = scores + key_mask
                    lse = r.stat[slot, head, here, :]
                probs = jnp.exp(scores - lse)
                pull = dot_rows(grad * head_mask[head], vals) - r.stat[slot, heads + head, here, :]
                products.append(dot_plain((probs * pull).astype(jnp.bfloat16), keys))
            r.dq[slot, here, :] = r.dq[slot, here, :] + pick_heads(products, lane_head)
            return unused

        lax.fori_loop(0, rows // chunk, part, 0)

    query_fold(0, r.near, block_of(r.kv_col, level, "keys"), True)
    other_grad_ref = None

    def own_earlier(from_level, unused):
        query_fold(0, r.near, block_of(r.kv_col, from_level, "keys"), False)
        return unused

    lax.fori_loop(0, level, own_earlier, 0)
    scatters[1].middle()
    own_grad_side().wait_recv()
    other_grad_ref = block_of(r.grad_oth, level, "grad")

    def other_stats(index, unused):
        here = pl.ds(pl.multiple_of(index * chunk, chunk), chunk)
        extended = other_grad_ref[here, :]
        for row in range(2 * heads):
            r.stat[1, row, here, :] = stat_column(extended, width, row)
        return unused

    lax.fori_loop(0, rows // chunk, other_stats, 0)

    def other_earlier(from_level, unused):
        query_fold(1, other_grad_ref, block_of(r.kv_col, from_level, "keys"), False)
        return unused

    lax.fori_loop(0, level + 1 - side, other_earlier, 0)
    r.dq_out[...] = r.dq[1].astype(jnp.bfloat16)
    dq_copy = pltpu.make_async_remote_copy(
        r.dq_out, r.dq_in, r.dq_sem.at[0], r.dq_sem.at[1], device_id=partner, device_id_type=MESH_ID
    )
    dq_copy.start()
    late.middle()

    own_block_ref = block_of(r.kv_col, level, "keys")

    def key_fold(query_ref, grad_ref, own):
        def part(index, unused):
            here = pl.ds(pl.multiple_of(index * chunk, chunk), chunk)
            keys = own_block_ref[here, :width]
            vals = own_block_ref[here, width:]
            query = query_ref[...]
            extended = grad_ref[...]
            if own:
                k_pos = index * chunk + lax.broadcasted_iota(jnp.int32, (chunk, rows), 0)
                q_pos = lax.broadcasted_iota(jnp.int32, (chunk, rows), 1)
                visible = (q_pos >= k_pos) & (r.doc_col[here, :] == r.doc_row[0:1, :])
            grad = extended[:, :width]
            stats = stat_rows(extended, width, 8)
            key_parts, val_parts = [], []
            for head in range(heads):
                scores = dot_rows(keys * head_mask[head], query)
                if own:
                    scores = jnp.where(visible, scores, NEGATIVE)
                probs = jnp.exp(scores - stats[head : head + 1, :])
                val_parts.append(dot_plain(probs.astype(jnp.bfloat16), grad))
                pull = dot_rows(vals * head_mask[head], grad) - stats[heads + head : heads + head + 1, :]
                key_parts.append(dot_plain((probs * pull).astype(jnp.bfloat16), query))
            r.dk[here, :] = r.dk[here, :] + pick_heads(key_parts, lane_head)
            r.dv[here, :] = r.dv[here, :] + pick_heads(val_parts, lane_head)
            return unused

        lax.fori_loop(0, rows // chunk, part, 0)

    @pl.when(side == 0)
    def _():
        key_fold(r.pair.at[1], block_of(r.grad_oth, level, "grad"), False)

    def later(from_level):
        grad_down(from_level, level).wait_recv()
        grad_side(from_level).start()
        key_fold(
            block_of(r.query_col, from_level, "query"), block_of(r.grad_col, from_level, "grad"), False
        )
        query_side(from_level).wait_recv()
        grad_side(from_level).wait_recv()
        key_fold(
            block_of(r.query_oth, from_level, "query"), block_of(r.grad_oth, from_level, "grad"), False
        )

    each_above(later)
    reaches = r.doc_col[...] >= (seq + 1) * rows
    r.dk[...] = jnp.where(reaches, r.dk[...], 0.0)
    r.dv[...] = jnp.where(reaches, r.dv[...], 0.0)
    key_fold(r.pair.at[0], r.near, True)
    dq_copy.wait()
    r.grads[...] = jnp.concatenate(
        [(r.dq[0] + r.dq_in[...].astype(jnp.float32)) * (DH**-0.5), r.dk[...], r.dv[...]], axis=1
    ).astype(jnp.bfloat16)

    for part in range(PARTS):
        third.start(part, dot_rows(r.grads[span(theirs(part)), :], r.qkv_w[...]))
        r.own[span(part * size), :] = dot_rows(r.grads[span(mine(part)), :], r.qkv_w[...])
    memory_part = jnp.concatenate(
        [
            jnp.concatenate(
                [jnp.zeros((width, width), jnp.float32), dot_columns(r.coeff[slot], r.mem_grad[...])], axis=1
            )
            for slot in range(4)
        ],
        axis=0,
    )
    weight_blocks(r.qkv_blocks, r.normed, r.grads[...], memory_part)
    scatters[3].start()
    for part in range(PARTS):
        third.middle(part, r.own[span(part * size), :])
    bias_row = column_sum(r.grads[...].astype(jnp.float32))
    r.small[7:8, :] = jnp.concatenate(
        [bias_row[:, :width], bias_row[:, 2 * width :], jnp.zeros((1, D - 2 * width), jnp.float32)], axis=1
    )
    scatters[2].middle()
    late.late()
    gain_sum = jnp.zeros((1, D), jnp.float32)
    offset_sum = jnp.zeros((1, D), jnp.float32)
    for part in range(PARTS):
        grad = third.result(part)
        nhat, scale = normalize(r.tok[span(mine(part)), :].astype(jnp.float32))
        gain_sum = gain_sum + column_sum(grad * nhat)
        offset_sum = offset_sum + column_sum(grad)
        out = r.mid[span(part * size), :] + norm_back(grad, nhat, scale, first_gain)
        r.tokens_out[span(mine(part)), :] = out.astype(jnp.bfloat16)
        token_share.copy(part, mine(part)).start()
    r.fold[0:1, :] = gain_sum
    r.fold[1:2, :] = offset_sum
    fold_copy = swap_with("core", r.fold, r.fold_in, (r.share_6, r.share_7), 0)
    fold_copy.start()
    scatters[3].middle()
    fold_copy.wait()
    r.small[0:5, :] = r.fold[0:5, :] + r.fold_in[0:5, :]
    small.start()
    scatters[0].finish(r.proj_share)
    scatters[1].finish(r.fc_share)
    small.middle()
    scatters[2].finish(r.out_share)
    scatters[3].finish(r.qkv_share)
    small.finish(r.small_out)
    late.finish()
    for part in range(PARTS):
        token_share.copy(part, theirs(part)).wait_recv()
        token_share.copy(part, mine(part)).wait_send()
        c_share.copy(part, mine(part)).wait_send()
        e_share.copy(part, mine(part)).wait_send()
    own_grad_side().wait_send()
    each_below(lambda other: query_down(level, other).wait_send())
    each_below(lambda other: grad_down(level, other).wait_send())
    each_above(lambda other: query_side(other).wait_send())
    each_above(lambda other: grad_side(other).wait_send())


def layer_back(levels, inputs):
    rows, width = inputs["heads"].shape
    heads = width // DH
    half = rows // 2
    size = half // PARTS
    hidden = inputs["fc_w"].shape[1]
    slab = D // (2 * levels)
    staged = levels > 8
    bf, fl = jnp.bfloat16, jnp.float32
    vmem = pl.BlockSpec(memory_space=pltpu.VMEM)
    far = pl.BlockSpec(memory_space=pl.ANY)
    dma = pltpu.SemaphoreType.DMA
    shape = jax.ShapeDtypeStruct
    outs = {
        "output": shape((rows, D), bf),
        "tokens_out": shape((rows, D), bf),
        "proj_share": shape((slab, hidden), fl),
        "fc_share": shape((slab, hidden), fl),
        "out_share": shape((slab, width), fl),
        "qkv_share": shape((slab, 3 * width), fl),
        "small_out": shape((16, D), fl),
    }
    gathered = {
        "query_col": ((levels, rows, width), bf),
        "query_oth": ((levels, rows, width), bf),
        "grad_col": ((levels, rows, LANES_OUT), bf),
        "grad_oth": ((levels, rows, LANES_OUT), bf),
    }
    scratch = {}
    out_specs = [vmem] * len(outs)
    if staged:
        for name, (dims, kind) in gathered.items():
            outs[name] = shape(dims, kind)
            out_specs.append(far)
        scratch["stage_query"] = pltpu.VMEM((rows, width), bf)
        scratch["stage_grad"] = pltpu.VMEM((rows, LANES_OUT), bf)
        scratch["stage_keys"] = pltpu.VMEM(inputs["kv_col"].shape[1:], bf)
        scratch["stage_sem"] = dma(())
    else:
        for name, (dims, kind) in gathered.items():
            scratch[name] = pltpu.VMEM(dims, kind)
    for name, dims, kind in (
        ("c", (rows, D), bf),
        ("e1", (rows, D), bf),
        ("u", (rows, hidden), bf),
        ("ef", (rows, hidden), bf),
        ("pull", (rows, hidden), fl),
        ("h1", (half, D), fl),
        ("own", (half, D), fl),
        ("base", (half, D), fl),
        ("mid", (half, D), fl),
        ("own_two", (half, D), fl),
        ("other_two", (half, D), bf),
        ("fold", (8, D), fl),
        ("fold_in", (8, D), fl),
        ("small", (16, D), fl),
        ("grad", (rows, width), bf),
        ("near", (rows, LANES_OUT), bf),
        ("far", (rows, LANES_OUT), bf),
        ("near_lse", (heads, rows, 1), fl),
        ("stat", (2, 2 * heads, rows, 1), fl),
        ("mem_acc", (NB, width), fl),
        ("pulls", (8, width), fl),
        ("mem_grad", (NB, 2 * width), bf),
        ("dq", (2, rows, width), fl),
        ("dk", (rows, width), fl),
        ("dv", (rows, width), fl),
        ("dq_out", (rows, width), bf),
        ("dq_in", (rows, width), bf),
        ("grads", (rows, 3 * width), bf),
        ("proj_blocks", (2 * levels, slab, hidden), bf),
        ("fc_blocks", (2 * levels, slab, hidden), bf),
        ("out_blocks", (2 * levels, slab, width), bf),
        ("qkv_blocks", (2 * levels, slab, 3 * width), bf),
    ):
        scratch[name] = pltpu.VMEM(dims, kind)

    def several(prefix, items):
        scratch.update({f"{prefix}_{index}": item for index, item in enumerate(items)})

    for name in ("first", "second", "third"):
        several(name, TpSum.scratch(PARTS, size, D))
    for name, columns in (("proj", hidden), ("fc", hidden), ("out", width), ("qkv", 3 * width)):
        several(name, Scatter.scratch(levels, slab, columns))
    several("small", SmallSum.scratch(levels, (16, D)))
    several("late", LateOutput.scratch(half, D))
    several("share", [dma((PARTS,))] * 8)
    for name in ("qd", "qs", "gd", "gs"):
        scratch[name + "_send"] = dma((levels,))
        scratch[name + "_recv"] = dma((levels,))
    scratch["dq_sem"] = dma((2,))
    names = [*inputs, *outs, *scratch]
    results = pl.pallas_call(
        functools.partial(back_kernel, levels, names),
        out_shape=tuple(outs.values()),
        in_specs=[far if staged and name == "kv_col" else vmem for name in inputs],
        out_specs=tuple(out_specs),
        scratch_shapes=list(scratch.values()),
        name="layer_back",
        compiler_params=pltpu.CompilerParams(
            collective_id=2, has_side_effects=True, vmem_limit_bytes=VMEM_LIMIT
        ),
    )(*inputs.values())
    return SimpleNamespace(**dict(zip(outs, results)))


def local(
    tokens,
    cotangent,
    past_states,
    doc_ids,
    cur_book,
    past_book,
    past_age,
    ln1_gain,
    ln1_bias,
    qkv_weight,
    qv_bias,
    out_weight,
    out_bias,
    ln2_gain,
    ln2_bias,
    fc_weight,
    fc_bias,
    proj_weight,
    proj_bias,
    mu_weight,
    sigma_weight,
):
    tok_rows = tokens.shape[0]
    heads_here = mu_weight.shape[0]
    head_cols = qkv_weight.shape[2]
    seq_count = lax.axis_size("seq")
    seq_index = lax.axis_index("seq")
    levels = seq_count // 2
    row_pad = ((0, 6), (0, 0))
    norm_rows = jnp.pad(jnp.stack([ln1_gain, ln1_bias]), row_pad)
    qkv_flat = qkv_weight.reshape(D, 3 * head_cols)
    bias_row = jnp.concatenate([qv_bias[0], jnp.zeros(head_cols, jnp.float32), qv_bias[1]])
    bias_rows = jnp.broadcast_to(bias_row[None], (8, 3 * head_cols))
    reaches = doc_ids >= (seq_index + 1) * tok_rows
    key_mask = jnp.where(reaches, 0.0, NEGATIVE).astype(jnp.bfloat16).reshape(2, tok_rows // 2)
    key_mask = jnp.pad(key_mask, ((0, 14), (0, 2 * head_cols - tok_rows // 2)))

    quarter = D // lax.axis_size("tp")
    columns = lax.dynamic_slice_in_dim(
        past_states, lax.axis_index("tp") * quarter, quarter, axis=1
    )
    half = SEG // 2
    marks = jnp.concatenate([past_book, past_age, jnp.zeros(14, jnp.int32)]).astype(jnp.bfloat16)
    past = jnp.concatenate(
        [
            jnp.concatenate([columns[:half], columns[half:]], axis=1),
            jnp.broadcast_to(marks[:, None], (16, 2 * quarter)),
        ]
    )
    book = jnp.broadcast_to(cur_book.astype(jnp.float32)[:, None], (8, 2 * quarter))
    spots = jnp.pad(jnp.stack([mu_weight, sigma_weight]), ((0, 0), (0, 8 - heads_here), (0, 0)))
    spots = spots.reshape(16, NB)
    table = jnp.asarray(np.stack(coefficient_tables(seq_count // BOOKS, NB, SEG), axis=1))

    normed, pair, kv_col, attended, lse, heads_out, coeff, memory, spot_rows = attention_forward(
        levels,
        tokens,
        norm_rows,
        qkv_flat,
        bias_rows,
        doc_ids,
        key_mask,
        past,
        book,
        spots,
        table,
    )
    vectors = jnp.pad(
        jnp.stack([ln2_gain, ln2_bias, out_bias, fc_bias, proj_bias, ln1_gain]), ((0, 2), (0, 0))
    )
    done = layer_back(
        levels,
        {
            "heads": heads_out,
            "tok": tokens,
            "cot": cotangent,
            "out_w": out_weight,
            "fc_w": fc_weight,
            "proj_w": proj_weight,
            "vec": vectors,
            "qkv_w": qkv_flat,
            "attended": attended,
            "lse": lse,
            "pair": pair,
            "kv_col": kv_col,
            "doc_col": doc_ids[:, None],
            "doc_row": doc_ids[None, :],
            "normed": normed,
            "coeff": coeff,
            "mem": memory,
            "spot_rows": spot_rows,
            "spots": spots,
        },
    )
    small = done.small_out
    return (
        done.output,
        done.tokens_out,
        done.qkv_share.reshape(-1, 3, head_cols),
        small[7, : 2 * head_cols].reshape(2, head_cols),
        done.out_share.T,
        small[4],
        done.fc_share,
        small[5],
        done.proj_share.T,
        small[6],
        small[0],
        small[1],
        small[2],
        small[3],
        small[8 : 8 + heads_here, :NB],
        small[8 + heads_here : 8 + 2 * heads_here, :NB],
    )


def solution(mesh):
    in_specs = (
        P("seq", None),
        P("seq", None),
        P("seq", None),
        P("seq"),
        P("seq"),
        P("seq"),
        P("seq"),
        P(),
        P(),
        P(None, None, "tp"),
        P(None, "tp"),
        P("tp", None),
        P(),
        P(),
        P(),
        P(None, "tp"),
        P("tp"),
        P("tp", None),
        P(),
        P("tp", None),
        P("tp", None),
    )
    out_specs = (
        P("seq", None),
        P("seq", None),
        P("seq", None, "tp"),
        P(None, "tp"),
        P("tp", "seq"),
        P(),
        P("seq", "tp"),
        P("tp"),
        P("tp", "seq"),
        P(),
        P(),
        P(),
        P(),
        P(),
        P("tp", None),
        P("tp", None),
    )
    return jax.shard_map(local, mesh=mesh, in_specs=in_specs, out_specs=out_specs, check_vma=False)
```

time: 260 us -> 235 us (0.904)
  waiting for transfers between devices: 19.2 us -> 0 us
    ppermute x2 -> x0, waiting for transfers between devices: 19.2 us -> none  [the longest x1 19.2 us: local(): query_oth = lax.ppermute(query_col, 'seq', swap)]
    pallas_call x1, Pallas kernels: 66 us -> 53.2 us  [attention_forward(): pl.pallas_call(functools.partial(forward_kernel, levels), out_shape=(jax....]
    pallas_call x3 -> x1, Pallas kernels: 138 us -> 150 us  [layer_back(): pl.pallas_call(functools.partial(back_kernel, levels, names), out_shape=t...]
    another operation x6, local copies, waits for them, and re-layouts: 0.06 us -> 3.48 us  [local(): jnp.stack([ln2_gain, ln2_bias, out_bias, fc_bias, proj_bias, ln1_gain])]
    convert_element_type x1 -> x0, other arithmetic: 2.64 us -> none  [shards(): return grad.astype(jnp.bfloat16).reshape(seq_count, D // seq_count, -1)]
    unnamed x40 -> x14, local copies, waits for them, and re-layouts: 6.06 us -> 6.96 us
  transfers between devices with their start and end apart: 2 -> 0, of which waited for: 1 -> 0; matrix products, arithmetic and copies ran while one was open for 2% -> 0% of each run, Pallas kernels for 12% -> 0%
where the time goes in v1:
time: 235 us; the launch traced here: 234 us
  Pallas kernels  203 us (86%)
  local copies, waits for them, and re-layouts  24.6 us (10%)
  other arithmetic  3.64 us (2%)
  between operations  2.74 us (1%)
    pallas_call x1, Pallas kernels, layer_back(): pl.pallas_call(functools.partial(back_kernel, levels, names), out_shape=t...  150 us
    pallas_call x1, Pallas kernels, attention_forward(): pl.pallas_call(functools.partial(forward_kernel, levels), out_shape=(jax....  53.2 us
    unnamed x14, local copies, waits for them, and re-layouts  6.96 us

profile of v1, /device:TPU:0, one launch (start us, length us, event | category | flops | bytes accessed | tf_op | source)
XLA Modules:
  0.0 234.1 jit_solution(7430989270272323695)
XLA Ops:
  0.6 0.0 copy-start
  2.7 0.7 select_convert_fusion
  3.4 0.1 pad_maximum_fusion.1
  3.5 0.8 fusion.2
  4.2 0.1 pad_maximum_fusion
  4.3 0.7 stack.37
  5.0 0.7 stack.38
  5.7 0.7 stack.45
  6.4 0.7 stack.43
  7.1 0.7 stack.44
  7.8 0.7 stack.46
  8.5 0.7 stack.47
  9.2 0.6 pad.19.refs_6_
  9.8 0.6 pad.17.key_mask_ref
  10.4 0.6 broadcast_in_dim.47.book_ref
  11.0 0.6 broadcast_in_dim.40.bias_ref
  11.6 0.6 select_maximum_fusion.1.norm_ref
  12.2 1.3 fusion.spot_ref.refs_18_
  13.6 1.2 constant_dynamic-slice_fusion
  14.7 0.8 maximum_maximum_fusion.past_ref
  15.6 1.5 copy.42.doc_col_ref.refs_12_
  17.1 0.0 copy-done
  17.1 1.3 copy.41.weight_ref.refs_7_
  18.4 53.2 %attention_forward.1 = (bf16[512,768]{1,0:T(8,128)(2,1)}, bf16[2,512,192]{2,1,0:T(8,128)(2,1)}, bf16[4,528,384]{2,1,0:T(8,128)(2,1)}, f32[512,192]{1,0:T(8,128)}...) custom-call(bf16[512,768]{1,0:T(8,128)(2,1)} %refs_1_.1, ...), custom_call_target="tpu_custom_call" | custom-call | tf_op jit(solution)/shard_map/attention_forward/pallas_call | solution.py:510
  71.6 150.0 %layer_back.1 = (bf16[512,768]{1,0:T(8,128)(2,1)}, bf16[512,768]{1,0:T(8,128)(2,1)}, f32[96,768]{1,0:T(8,128)}, f32[96,768]{1,0:T(8,128)}, f32[96,192]{1,0:T(8,1...) custom-call(bf16[512,192]{1,0:T(8,128)(2,1)} %get-tuple-element.32.refs_0_, bf16[512,768]{1,0:T(8,128)(2,1)} %refs_1_.1, ...), custom_call_target="tpu_custom_call" | custom-call | tf_op jit(solution)/shard_map/layer_back/pallas_call | solution.py:1378
  221.6 0.0 copy-start.1
  221.6 0.8 slice_reduce_fusion.7
  222.4 0.7 reshape_squeeze.3
  223.0 1.4 fusion.1
  224.4 1.7 slice_reduce_fusion
  226.1 1.6 copy.47
  227.7 1.1 copy.45
  228.8 0.9 copy.46
  229.7 0.0 copy-start.3
  229.7 0.0 copy-start.2
  229.7 2.1 copy.55
  231.8 0.0 copy-done.1
  231.8 0.9 copy.56
  232.7 0.0 copy-done.3
  232.7 0.7 copy.57
  233.4 0.0 copy-done.2
  233.4 0.7 copy.58
  (4 shorter events, 0.1 us)
Async XLA Ops:
  0.6 16.5 %copy-start = (bf16[768,3,192]{0,2,1:T(8,128)(2,1)S(1)}, bf16[768,3,192]{0,2,1:T(8,128)(2,1)}, u32[]{:S(2)}) copy-start(bf16[768,3,192]{0,2,1:T(8,128)(2,1)} %param.31) | copy-start | bytes 2654212
  221.6 10.3 %copy-start.1 = (bf16[512,768]{1,0:T(8,128)(2,1)S(1)}, bf16[512,768]{1,0:T(8,128)(2,1)}, u32[]{:S(2)}) copy-start(bf16[512,768]{1,0:T(8,128)(2,1)} %get-tuple-element.110) | copy-start | bytes 2359300
  229.7 3.0 %copy-start.3 = (f32[96,768]{1,0:T(8,128)S(1)}, f32[96,768]{1,0:T(8,128)}, u32[]{:S(2)}) copy-start(f32[96,768]{1,0:T(8,128)} %get-tuple-element.115) | copy-start | bytes 884740
  229.7 3.7 %copy-start.2 = (f32[96,768]{1,0:T(8,128)S(1)}, f32[96,768]{1,0:T(8,128)}, u32[]{:S(2)}) copy-start(f32[96,768]{1,0:T(8,128)} %get-tuple-element.47) | copy-start | bytes 884740
